TPU v7x, 512 devices: a whole 4x8x8 slice. The times are simulated.
512 devices in a mesh: dp: 64 (over y, x, z_lo), seq: 8 (over z_hi, core).
Axes of the slice: x: 4, y: 8, z: 8 (z_hi: 4, z_lo: 2; z = z_hi * 2 + z_lo), core: 2. Of those that a mesh axis runs over, the one named last changes fastest.
Arguments:
- queries: bfloat16 [65536, 2048], P(('dp', 'seq')), may hold values from -12 to 12
- keys: bfloat16 [65536, 2048], P(('dp', 'seq')), may hold values from -6 to 6
- values: bfloat16 [65536, 2048], P(('dp', 'seq')), may hold values from -6 to 6
- d_queries: bfloat16 [65536, 2048], P(('dp', 'seq')), may hold values from -6 to 6
- d_keys: bfloat16 [65536, 2048], P(('dp', 'seq')), may hold values from -6 to 6
- d_values: bfloat16 [65536, 2048], P(('dp', 'seq')), may hold values from -6 to 6
- out_weight: bfloat16 [2048, 3072], P('dp', 'seq'), may hold values from -0.125 to 0.125
- tangent_coef: float32 [64], P('dp'), may hold values from 0.5 to 2
- loss_weight: float32 [64], P('dp'), may hold values from 0.1 to 3
Outputs:
- weight_grad: float32 [2048, 3072], P('dp', 'seq')
All inputs are finite; a program needn't handle non-finite values.
Results may differ from a plain program's by a relative error of at most 0.014.
Values may be sent and summed in bfloat16 or wider, within the bound.
No kernel may reach another device: no remote copies, remote signals or barrier semaphores. Data moves between devices by JAX's collectives and lax.ppermute only.
A program may use at most 64 MiB of HBM per device.

v0:
```python
import jax
import jax.numpy as jnp
from jax import lax
from jax.sharding import PartitionSpec as P

HEAD = 128


loss_scale = 64.0


def blocked(x, size):
    return x.reshape((x.shape[0] // size, size) + x.shape[1:])


def unblocked(x):
    return x.reshape((x.shape[0] * x.shape[1],) + x.shape[2:])


def soft_rows(q_block, k_all, scale):
    scores = jnp.einsum("qhd,khd->hqk", q_block, k_all, preferred_element_type=jnp.float32) * scale
    peak = jnp.max(scores, axis=-1, keepdims=True)
    expo = jnp.exp(scores - peak)
    return expo / jnp.sum(expo, axis=-1, keepdims=True)


def attend_rows(probs, v_all):
    low = probs.astype(jnp.bfloat16)
    return jnp.einsum("hqk,khd->qhd", low, v_all, preferred_element_type=jnp.float32).astype(
        jnp.bfloat16
    )


def tangent_rows(probs, q_block, dq_block, k_all, dk_all, v_all, dv_all, scale):
    d_scores = jnp.einsum("qhd,khd->hqk", dq_block, k_all, preferred_element_type=jnp.float32)
    d_scores = (
        d_scores + jnp.einsum("qhd,khd->hqk", q_block, dk_all, preferred_element_type=jnp.float32)
    ) * scale
    d_probs = probs * (d_scores - jnp.sum(probs * d_scores, axis=-1, keepdims=True))
    d_low = d_probs.astype(jnp.bfloat16)
    low = probs.astype(jnp.bfloat16)
    first = jnp.einsum("hqk,khd->qhd", d_low, v_all, preferred_element_type=jnp.float32)
    second = jnp.einsum("hqk,khd->qhd", low, dv_all, preferred_element_type=jnp.float32)
    return (first + second).astype(jnp.bfloat16)


def shards(
    queries, keys, values, d_queries, d_keys, d_values, out_weight, tangent_coef, loss_weight
):
    seq_count = lax.axis_size("seq")
    length = queries.shape[0] * seq_count
    width_dev = queries.shape[1] // seq_count
    heads_dev = width_dev // HEAD
    block = min(512, length)
    scale = 1.0 / HEAD**0.5

    def to_heads(x):
        return x.reshape(length, heads_dev, HEAD)

    q_all, k_all, v_all = (
        lax.all_to_all(queries, "seq", split_axis=1, concat_axis=0, tiled=True),
        lax.all_to_all(keys, "seq", split_axis=1, concat_axis=0, tiled=True),
        lax.all_to_all(values, "seq", split_axis=1, concat_axis=0, tiled=True),
    )
    q3, k3, v3 = (to_heads(q_all), to_heads(k_all), to_heads(v_all))

    def forward(q_block):
        probs = soft_rows(q_block, k3, scale)
        return (probs, attend_rows(probs, v3))

    prob_blocks, out_blocks = lax.map(forward, blocked(q3, block))
    dq_all, dk_all, dv_all = (
        lax.all_to_all(d_queries, "seq", split_axis=1, concat_axis=0, tiled=True),
        lax.all_to_all(d_keys, "seq", split_axis=1, concat_axis=0, tiled=True),
        lax.all_to_all(d_values, "seq", split_axis=1, concat_axis=0, tiled=True),
    )
    dq3, dk3, dv3 = (to_heads(dq_all), to_heads(dk_all), to_heads(dv_all))

    def tangent(items):
        return tangent_rows(items[0], items[1], items[2], k3, dk3, v3, dv3, scale)

    tan_blocks = lax.map(tangent, (prob_blocks, blocked(q3, block), blocked(dq3, block)))
    attended = unblocked(out_blocks).reshape(length, width_dev)
    d_attended = unblocked(tan_blocks).reshape(length, width_dev)
    whole_out, whole_tan = (
        lax.all_gather(attended, "seq", axis=1, tiled=True),
        lax.all_gather(d_attended, "seq", axis=1, tiled=True),
    )
    coef = tangent_coef[0]
    weight = loss_weight[0]
    mixed = (whole_out.astype(jnp.float32) + coef * whole_tan.astype(jnp.float32)).astype(
        jnp.bfloat16
    )
    projected = jnp.dot(
        mixed,
        lax.all_gather(out_weight, "dp", axis=0, tiled=True),
        preferred_element_type=jnp.float32,
    )
    residual_grad = (weight * projected).astype(jnp.bfloat16)
    partial_term = jnp.einsum(
        "sf,sc->fc", whole_out, residual_grad, preferred_element_type=jnp.float32
    )
    summed = lax.psum_scatter(partial_term, "dp", scatter_dimension=0, tiled=True)
    total_tokens = length * lax.axis_size("dp")
    return summed * (loss_scale / total_tokens**0.5)


def solution(mesh):
    placed = (
        P(("dp", "seq"), None),
        P(("dp", "seq"), None),
        P(("dp", "seq"), None),
        P(("dp", "seq"), None),
        P(("dp", "seq"), None),
        P(("dp", "seq"), None),
        P("dp", "seq"),
        P("dp"),
        P("dp"),
    )
    return jax.shard_map(
        shards, mesh=mesh, in_specs=placed, out_specs=P("dp", "seq"), check_vma=False
    )
```

profile of v0, /device:TPU:128, one launch (start us, length us, event | category | flops | bytes accessed | tf_op | source)
XLA Modules:
  0.0 868.9 jit_solution(2651828491635451152)
XLA Ops:
  6.5 2.2 copy.28
  8.7 9.0 %all-to-all-start.1 = ((bf16[128,8,256]{0,2,1:T(8,128)(2,1)}), bf16[128,8,256]{0,2,1:T(8,128)(2,1)S(1)}, u32[]{:S(2)}, u32[]{:S(2)}) async-start(bf16[128,8,256]{0,2,1:T(8,128)(2,1)} %bitcast.10), calls=%async_computation.1 | async-start | bytes 1048576 | tf_op jit(solution)/shard_map/all_to_all | solution.py:62
  17.8 2.1 copy.30
  19.9 13.9 %all-to-all-done.1 = bf16[128,8,256]{0,2,1:T(8,128)(2,1)S(1)} async-done(((bf16[128,8,256]{0,2,1:T(8,128)(2,1)}), bf16[128,8,256]{0,2,1:T(8,128)(2,1)S(1)}, u32[]{:S(2)}, u32[]{:S(2)}) %all-to-all-start.1) | async-done | bytes 524320 | tf_op jit(solution)/shard_map/all_to_all | solution.py:62
  33.8 5.8 all-to-all-start.2
  40.4 15.1 %all-to-all-done.2 = bf16[128,8,256]{0,2,1:T(8,128)(2,1)S(1)} async-done(((bf16[128,8,256]{0,2,1:T(8,128)(2,1)}), bf16[128,8,256]{0,2,1:T(8,128)(2,1)S(1)}, u32[]{:S(2)}, u32[]{:S(2)}) %all-to-all-start.2) | async-done | bytes 524320 | tf_op jit(solution)/shard_map/all_to_all | solution.py:63
  55.5 5.1 all-to-all-start
  61.6 14.6 %all-to-all-done = bf16[128,8,256]{2,0,1:T(8,128)(2,1)S(1)} async-done(((bf16[128,8,256]{2,0,1:T(8,128)(2,1)}), bf16[128,8,256]{2,0,1:T(8,128)(2,1)S(1)}, u32[]{:S(2)}, u32[]{:S(2)}) %all-to-all-start) | async-done | bytes 524320 | tf_op jit(solution)/shard_map/all_to_all | solution.py:61
  76.1 6.1 all-to-all-start.4
  82.2 1.1 copy.39
  83.3 15.0 %all-to-all-done.4 = bf16[128,8,256]{0,2,1:T(8,128)(2,1)S(1)} async-done(((bf16[128,8,256]{0,2,1:T(8,128)(2,1)}), bf16[128,8,256]{0,2,1:T(8,128)(2,1)S(1)}, u32[]{:S(2)}, u32[]{:S(2)}) %all-to-all-start.4) | async-done | bytes 524320 | tf_op jit(solution)/shard_map/all_to_all | solution.py:74
  98.3 5.3 all-to-all-start.5
  105.5 1.0 reshape.39
  106.5 1.3 copy.33
  109.2 1.3 copy.34
  110.7 8.8 %all-to-all-done.5 = bf16[128,8,256]{0,2,1:T(8,128)(2,1)S(1)} async-done(((bf16[128,8,256]{0,2,1:T(8,128)(2,1)}), bf16[128,8,256]{0,2,1:T(8,128)(2,1)S(1)}, u32[]{:S(2)}, u32[]{:S(2)}) %all-to-all-start.5) | async-done | bytes 524320 | tf_op jit(solution)/shard_map/all_to_all | solution.py:75
  119.5 4.3 all-to-all-start.3
  123.8 1.1 broadcast.12.clone2
  124.9 20.0 %while.22 = (s32[]{:T(128)}, f32[2,2,512,1024]{3,2,1,0:T(8,128)}, bf16[2,512,2,128]{3,2,1,0:T(2,128)(2,1)}, bf16[2,512,2,128]{3,1,2,0:T(8,128)(2,1)S(1)}, bf16[1...) while((s32[]{:T(128)}, f32[2,2,512,1024]{3,2,1,0:T(8,128)}, ...), condition=%wide.region_3.4_spmd, body=%wide.region_0.3_spmd.sunk | while | flops 543294464 | bytes 39858856 | solution.py:71
  124.9 3.4 fusion.93
  128.3 3.1 fusion.94
  132.5 2.4 bitcast_dynamic-update-slice_fusion.2
  134.8 3.4 fusion.93
  138.2 3.1 fusion.94
  142.4 2.4 bitcast_dynamic-update-slice_fusion.2
  144.9 1.2 copy.38
  146.1 2.1 reshape.41
  148.1 1.3 copy.44
  149.4 1.2 copy.40
  150.6 2.1 reshape.42
  152.7 1.3 copy.46
  154.9 1.2 reshape_reshape.15
  156.0 1.1 broadcast.12.clone
  157.1 22.1 %while.23 = (s32[]{:T(128)}, bf16[2,512,2,128]{3,2,1,0:T(2,128)(2,1)}, f32[2,2,512,1024]{3,2,1,0:T(8,128)}, bf16[2,512,2,128]{3,2,1,0:T(2,128)(2,1)S(1)}, bf16[1...) while((s32[]{:T(128)}, ...), condition=%wide.region_6.7_spmd, body=%wide.region_4.6_spmd.sunk | while | flops 1081342976 | bytes 32254568 | solution.py:82
  158.0 3.2 fusion.102
  161.2 2.9 fusion.100
  164.1 3.1 fusion.103
  169.1 3.2 fusion.102
  172.2 2.9 fusion.100
  175.1 3.1 fusion.103
  179.2 2.0 copy.65
  181.3 1.9 copy.66
  184.8 227.2 %all-gather.8.cloned.1.call-done = bf16[2048,384]{1,0:T(8,128)(2,1)} async-done(((bf16[32,384]{1,0:T(8,128)(2,1)}), bf16[2048,384]{1,0:T(8,128)(2,1)}) %all-gather.8.cloned.1.call-update) | async-done | bytes 1572880 | tf_op jit(solution)/shard_map/all_gather | solution.py:96
  412.0 57.3 %all-gather.6.cloned.1.call-done = bf16[1024,2048]{1,0:T(8,128)(2,1)} async-done(((bf16[1024,256]{1,0:T(8,128)(2,1)}), bf16[1024,2048]{1,0:T(8,128)(2,1)}) %all-gather.6.cloned.1.call-update) | async-done | bytes 4194320 | tf_op jit(solution)/shard_map/all_gather | solution.py:87
  469.3 60.1 %all-gather.4.cloned.1.call-done = bf16[1024,2048]{1,0:T(8,128)(2,1)} async-done(((bf16[1024,256]{1,0:T(8,128)(2,1)}), bf16[1024,2048]{1,0:T(8,128)(2,1)}) %all-gather.4.cloned.1.call-update) | async-done | bytes 4194320 | tf_op jit(solution)/shard_map/all_gather | solution.py:86
  529.4 11.3 %fusion.59 = f32[2048,384]{1,0:T(8,128)} fusion(bf16[1024,2048]{1,0:T(8,128)(2,1)} %all-gather.4.cloned.1.call-done, bf16[2048,384]{1,0:T(8,128)(2,1)} %all-gather.8.cloned.1.call-done, bf16[1024,2048]{1,0:T(8,128)(2,1)} %all-gather.6.cloned.1.call-done, f32[]{:T(128)} %bitcast.129, f32[]{:T(128)} %bitcast.130), kind=kOutput, calls=%fused_computation.52 | convolution fusion | flops 3232497664 | bytes 13107208 | tf_op jit(solution)/shard_map/sf,sc->fc/dot_general | solution.py:100
  540.7 320.3 %reduce-scatter.2.cloned.1.call-done = f32[32,384]{1,0:T(8,128)} async-done(((f32[2048,384]{1,0:T(8,128)}), f32[32,384]{1,0:T(8,128)}) %reduce-scatter.2.cloned.1.call-update) | async-done | bytes 49168 | tf_op jit(solution)/shard_map/reduce_scatter | solution.py:103
  861.0 1.4 broadcast_multiply_fusion
  (48 shorter events, 12.4 us)
Async XLA Ops:
  6.5 33.0 %copy-start.4 = (bf16[128,2048]{1,0:T(8,128)(2,1)S(1)}, bf16[128,2048]{1,0:T(8,128)(2,1)}, u32[]{:S(2)}) copy-start(bf16[128,2048]{1,0:T(8,128)(2,1)} %param.13) | copy-start | bytes 1572868
  6.5 54.0 %copy-start.5 = (bf16[128,2048]{1,0:T(8,128)(2,1)S(1)}, bf16[128,2048]{1,0:T(8,128)(2,1)}, u32[]{:S(2)}) copy-start(bf16[128,2048]{1,0:T(8,128)(2,1)} %param.17) | copy-start | bytes 1572868
  6.5 75.7 %copy-start.6 = (bf16[128,2048]{1,0:T(8,128)(2,1)S(1)}, bf16[128,2048]{1,0:T(8,128)(2,1)}, u32[]{:S(2)}) copy-start(bf16[128,2048]{1,0:T(8,128)(2,1)} %param.18) | copy-start | bytes 1572868
  8.7 25.1 %all-to-all-start.1 = ((bf16[128,8,256]{0,2,1:T(8,128)(2,1)}), bf16[128,8,256]{0,2,1:T(8,128)(2,1)S(1)}, u32[]{:S(2)}, u32[]{:S(2)}) async-start(bf16[128,8,256]{0,2,1:T(8,128)(2,1)} %bitcast.10), calls=%async_computation.1 | async-start | bytes 1048576 | tf_op jit(solution)/shard_map/all_to_all | solution.py:62
  17.8 86.5 %copy-start.7 = (bf16[128,2048]{1,0:T(8,128)(2,1)S(1)}, bf16[128,2048]{1,0:T(8,128)(2,1)}, u32[]{:S(2)}) copy-start(bf16[128,2048]{1,0:T(8,128)(2,1)} %param.16) | copy-start | bytes 1572868
  33.8 21.7 %all-to-all-start.2 = ((bf16[128,8,256]{0,2,1:T(8,128)(2,1)}), bf16[128,8,256]{0,2,1:T(8,128)(2,1)S(1)}, u32[]{:S(2)}, u32[]{:S(2)}) async-start(bf16[128,8,256]{0,2,1:T(8,128)(2,1)} %bitcast.12), calls=%async_computation.2 | async-start | bytes 1048576 | tf_op jit(solution)/shard_map/all_to_all | solution.py:63
  55.5 20.7 %all-to-all-start = ((bf16[128,8,256]{2,0,1:T(8,128)(2,1)}), bf16[128,8,256]{2,0,1:T(8,128)(2,1)S(1)}, u32[]{:S(2)}, u32[]{:S(2)}) async-start(bf16[128,8,256]{2,0,1:T(8,128)(2,1)} %bitcast.98), calls=%async_computation | async-start | bytes 1048576 | tf_op jit(solution)/shard_map/all_to_all | solution.py:61
  76.1 22.1 %all-to-all-start.4 = ((bf16[128,8,256]{0,2,1:T(8,128)(2,1)}), bf16[128,8,256]{0,2,1:T(8,128)(2,1)S(1)}, u32[]{:S(2)}, u32[]{:S(2)}) async-start(bf16[128,8,256]{0,2,1:T(8,128)(2,1)} %bitcast.17), calls=%async_computation.4 | async-start | bytes 1048576 | tf_op jit(solution)/shard_map/all_to_all | solution.py:74
  98.3 21.3 %all-to-all-start.5 = ((bf16[128,8,256]{0,2,1:T(8,128)(2,1)}), bf16[128,8,256]{0,2,1:T(8,128)(2,1)S(1)}, u32[]{:S(2)}, u32[]{:S(2)}) async-start(bf16[128,8,256]{0,2,1:T(8,128)(2,1)} %bitcast.19), calls=%async_computation.5 | async-start | bytes 1048576 | tf_op jit(solution)/shard_map/all_to_all | solution.py:75
  103.5 308.5 %all-gather.8.cloned.1.call-start = ((), (), s32[]{:S(2)}) async-start(), calls=%async_computation.9 | async-start | bytes 1597440 | tf_op jit(solution)/shard_map/all_gather | solution.py:96
  119.5 34.5 %all-to-all-start.3 = ((bf16[128,8,256]{2,0,1:T(8,128)(2,1)}), bf16[128,8,256]{2,0,1:T(8,128)(2,1)S(1)}, u32[]{:S(2)}, u32[]{:S(2)}) async-start(bf16[128,8,256]{2,0,1:T(8,128)(2,1)} %bitcast.97), calls=%async_computation.3 | async-start | bytes 1048576 | tf_op jit(solution)/shard_map/all_to_all | solution.py:73
  123.8 345.4 %all-gather.6.cloned.1.call-start = ((), (), s32[]{:S(2)}) async-start(), calls=%async_computation.8 | async-start | bytes 4718592 | tf_op jit(solution)/shard_map/all_gather | solution.py:87
  128.3 3.1 copy-start.2
  128.3 4.2 copy-start
  131.7 0.8 copy-start.3
  138.2 3.1 copy-start.2
  138.2 4.2 copy-start
  141.6 0.8 copy-start.3
  154.0 0.8 copy-start.1
  181.2 348.1 %all-gather.4.cloned.1.call-start = ((), (), s32[]{:S(2)}) async-start(), calls=%async_computation.7 | async-start | bytes 4718592 | tf_op jit(solution)/shard_map/all_gather | solution.py:86
  183.2 677.7 %reduce-scatter.2.cloned.1.call-start = ((), (), s32[]{:S(2)}) async-start(), calls=%async_computation.10 | async-start | bytes 3194880 | tf_op jit(solution)/shard_map/reduce_scatter | solution.py:103
Sparse Core Ops, SparseCore 0:
  106.4 305.5 all-gather.7
  414.1 55.1 all-gather.5
  471.4 57.9 all-gather.3
  540.8 320.0 reduce-scatter.1
where the time goes:
time: 870 us; the launch traced here: 869 us
  waiting for transfers between devices  733 us (84%)
  matrix products  43.9 us (5%)
  starting transfers between devices  35.8 us (4%)
  local copies, waits for them, and re-layouts  35.3 us (4%)
  between operations  14.5 us (2%)
    reduce_scatter x1, waiting for transfers between devices, shards(): lax.psum_scatter(partial_term, 'dp', scatter_dimension=0, tiled=True)  320 us
    all_gather x1, waiting for transfers between devices, shards(): lax.all_gather(out_weight, 'dp', axis=0, tiled=True)  227 us
    all_gather x1, waiting for transfers between devices, shards(): lax.all_gather(attended, 'seq', axis=1, tiled=True)  60.1 us
    all_gather x1, waiting for transfers between devices, shards(): lax.all_gather(d_attended, 'seq', axis=1, tiled=True)  57.3 us
  transfers between devices with their start and end apart: 10, of which 9 were waited for; matrix products, arithmetic and copies ran while one was open for 8% of the time, Pallas kernels for 0%

commit v1 on v0

v1 whole, which is shorter than its diff:
```python
import functools

import jax
import jax.numpy as jnp
from jax import lax
from jax.experimental import pallas as pl
from jax.experimental.pallas import tpu as pltpu
from jax.sharding import Mesh
from jax.sharding import PartitionSpec as P

HEAD = 128
LOSS_SCALE = 64.0
ROWS = 256
SEQ = ("zh", "core")
DP = ("y", "x", "zl")
NT = (((1,), (1,)), ((), ()))


def dot(a, b):
    return jnp.dot(a, b, preferred_element_type=jnp.float32)


def dot_nt(a, b):
    return lax.dot_general(a, b, NT, preferred_element_type=jnp.float32)


def flat(ref):
    return ref[...].reshape(-1, HEAD)


def probs_of(q, k, scale):
    scores = dot_nt(q, k) * scale
    expo = jnp.exp(scores - jnp.max(scores, axis=-1, keepdims=True))
    return expo / jnp.sum(expo, axis=-1, keepdims=True)


def forward_kernel(scale, q_ref, k_ref, v_ref, at_ref):
    low = probs_of(flat(q_ref), flat(k_ref), scale).astype(jnp.bfloat16)
    at_ref[...] = dot(low, flat(v_ref)).T.astype(jnp.bfloat16)


def tangent_kernel(
    scale, coef_ref, q_ref, k_ref, v_ref, dq_ref, dk_ref, dv_ref, mixed_ref
):
    q, k, v = flat(q_ref), flat(k_ref), flat(v_ref)
    probs = probs_of(q, k, scale)
    low = probs.astype(jnp.bfloat16)
    left = jnp.concatenate([flat(dq_ref), q], axis=1)
    right = jnp.concatenate([k, flat(dk_ref)], axis=1)
    d_scores = dot_nt(left, right) * scale
    shift = jnp.sum(probs * d_scores, axis=-1, keepdims=True)
    d_low = (probs * (d_scores - shift)).astype(jnp.bfloat16)
    tangent = (dot(d_low, v) + dot(low, flat(dv_ref))).astype(jnp.bfloat16)
    attended = dot(low, v).astype(jnp.bfloat16)
    mixed_ref[...] = (
        attended.astype(jnp.float32) + coef_ref[0] * tangent.astype(jnp.float32)
    ).astype(jnp.bfloat16)


def attention_specs(seq_count, tokens, arrays):
    per = ROWS // tokens
    query = lambda n: pl.BlockSpec((per, 1, tokens, HEAD), lambda h, i: (i, n, 0, h))
    whole = lambda n: pl.BlockSpec((seq_count, 1, tokens, HEAD), lambda h, i: (0, n, 0, h))
    return [query(0), whole(1), whole(2)] * arrays


def attend(qkv, scale):
    seq_count, _, tokens, width = qkv.shape
    length = seq_count * tokens
    return pl.pallas_call(
        functools.partial(forward_kernel, scale),
        grid=(width // HEAD, length // ROWS),
        in_specs=attention_specs(seq_count, tokens, 1),
        out_specs=pl.BlockSpec((HEAD, ROWS), lambda h, i: (h, i)),
        out_shape=jax.ShapeDtypeStruct((width, length), jnp.bfloat16),
        compiler_params=pltpu.CompilerParams(vmem_limit_bytes=32 << 20),
        cost_estimate=pl.CostEstimate(
            flops=8 * length * length * width, bytes_accessed=8 << 20, transcendentals=length * length * 2
        ),
        name="attend",
    )(qkv, qkv, qkv)


def attend_tangent(coef, qkv, d_qkv, scale):
    seq_count, _, tokens, width = qkv.shape
    length = seq_count * tokens
    return pl.pallas_call(
        functools.partial(tangent_kernel, scale),
        grid=(width // HEAD, length // ROWS),
        in_specs=[pl.BlockSpec(memory_space=pltpu.SMEM)] + attention_specs(seq_count, tokens, 2),
        out_specs=pl.BlockSpec((ROWS, HEAD), lambda h, i: (i, h)),
        out_shape=jax.ShapeDtypeStruct((length, width), jnp.bfloat16),
        compiler_params=pltpu.CompilerParams(vmem_limit_bytes=32 << 20),
        cost_estimate=pl.CostEstimate(
            flops=14 * length * length * width, bytes_accessed=8 << 20, transcendentals=length * length * 2
        ),
        name="tangent",
    )(coef, qkv, qkv, qkv, d_qkv, d_qkv, d_qkv)


def gram_kernel(count, weight_ref, place_ref, *refs):
    mixed_ref, out_ref = refs[-2], refs[-1]
    for n in range(count):
        out_ref[place_ref[n]] = weight_ref[0] * dot(refs[n][...], mixed_ref[...])


def gram(weight, place, blocks, mixed):
    count = len(blocks)
    rows, cols = blocks[0].shape[0], mixed.shape[1]
    smem = pl.BlockSpec(memory_space=pltpu.SMEM)
    vmem = pl.BlockSpec(memory_space=pltpu.VMEM)
    return pl.pallas_call(
        functools.partial(gram_kernel, count),
        in_specs=[smem, smem] + [vmem] * (count + 1),
        out_specs=vmem,
        out_shape=jax.ShapeDtypeStruct((count, rows, cols), jnp.float32),
        compiler_params=pltpu.CompilerParams(vmem_limit_bytes=32 << 20),
        name="gram",
    )(weight, place, *blocks, mixed)


def finish_kernel(factor, g_ref, w_ref, out_ref):
    total = jnp.zeros(out_ref.shape, jnp.float32)
    for n in range(g_ref.shape[0]):
        high = g_ref[n].astype(jnp.bfloat16)
        rest = (g_ref[n] - high.astype(jnp.float32)).astype(jnp.bfloat16)
        total = total + dot(high, w_ref[n]) + dot(rest, w_ref[n])
    out_ref[...] = total * factor


def finish(g, w, factor):
    return pl.pallas_call(
        functools.partial(finish_kernel, factor),
        out_shape=jax.ShapeDtypeStruct((g.shape[1], w.shape[2]), jnp.float32),
        compiler_params=pltpu.CompilerParams(vmem_limit_bytes=32 << 20),
        name="finish",
    )(g, w)


def shift(x, step):
    n = lax.axis_size("zh")
    return lax.ppermute(x, "zh", [(i, (i + step) % n) for i in range(n)])


def swap(x):
    return lax.ppermute(x, "core", [(0, 1), (1, 0)])


def gather_blocks(x):
    half = x.shape[0] // 2
    before, after = shift(x, 1), shift(x, -1)
    far = jnp.concatenate([shift(before[:half], 1), shift(after[half:], -1)], axis=0)
    own = [x, before, after, far]
    other = [swap(b) for b in own]
    zh, core = lax.axis_index("zh"), lax.axis_index("core")
    places = []
    for c in (core, 1 - core):
        for step in (0, 3, 1, 2):
            places.append(((zh + step) % 4) * 2 + c)
    return own + other, jnp.stack(places).astype(jnp.int32)


def to_heads(arrays, seq_count):
    stacked = jnp.stack(
        [x.reshape(x.shape[0], seq_count, -1).transpose(1, 0, 2) for x in arrays], axis=1
    )
    return lax.all_to_all(stacked, SEQ, split_axis=0, concat_axis=0, tiled=True)


def shards(
    queries, keys, values, d_queries, d_keys, d_values, out_weight, tangent_coef, loss_weight
):
    seq_count = lax.axis_size(SEQ)
    dp_count = lax.axis_size(DP)
    length = queries.shape[0] * seq_count
    scale = 1.0 / HEAD**0.5

    qkv = to_heads((queries, keys, values), seq_count)
    d_qkv = to_heads((d_queries, d_keys, d_values), seq_count)

    weight_all = lax.all_gather(out_weight, "zl", axis=0, tiled=True)
    weight_all = lax.all_gather(weight_all, "x", axis=0, tiled=True)
    weight_all = lax.all_gather(weight_all, "y", axis=0, tiled=True)

    attended_t = attend(qkv, scale)
    blocks, place = gather_blocks(attended_t)
    mixed = attend_tangent(tangent_coef, qkv, d_qkv, scale)
    term = gram(loss_weight, place, blocks, mixed)
    width = mixed.shape[1]
    parts = lax.all_to_all(
        term.reshape(dp_count, -1, width), DP, split_axis=0, concat_axis=0, tiled=True
    )
    summed = jnp.sum(parts, axis=0)
    rows = lax.all_to_all(
        jnp.broadcast_to(summed[None], (seq_count,) + summed.shape),
        SEQ,
        split_axis=0,
        concat_axis=0,
        tiled=True,
    )
    total_tokens = length * dp_count
    return finish(
        rows, weight_all.reshape(seq_count, width, -1), LOSS_SCALE / total_tokens**0.5
    )


def solution(mesh):
    split = Mesh(mesh.devices.reshape(8, 4, 2, 4, 2), DP + SEQ)
    tokens = P(DP + SEQ, None)
    placed = (tokens,) * 6 + (P(DP, SEQ), P(DP), P(DP))
    return jax.shard_map(
        shards, mesh=split, in_specs=placed, out_specs=P(DP, SEQ), check_vma=False
    )
```

time: 870 us -> 262 us (0.30)
  the two profiles are of different devices: /device:TPU:128 before, /device:TPU:1 now
where the time goes in v1:
time: 262 us; the launch traced here: 261 us
  waiting for transfers between devices  115 us (44%)
  starting transfers between devices  72.2 us (28%)
  Pallas kernels  24.5 us (9%)
  blocking collectives  17.7 us (7%)
  between operations  15 us (6%)
  local copies, waits for them, and re-layouts  12.8 us (5%)
  other arithmetic  3.82 us (1%)
    ppermute x4, waiting for transfers between devices, shift(): return lax.ppermute(x, 'zh', [(i, (i + step) % n) for i in range(n)])  45.7 us
    all_to_all x1, waiting for transfers between devices, shards(): lax.all_to_all(term.reshape(dp_count, -1, width), DP, split_axis=0, conca...  34.9 us
    all_to_all x2, starting transfers between devices, to_heads(): return lax.all_to_all(stacked, SEQ, split_axis=0, concat_axis=0, tiled=True)  27.1 us
    all_to_all x2, waiting for transfers between devices, to_heads(): return lax.all_to_all(stacked, SEQ, split_axis=0, concat_axis=0, tiled=True)  22.4 us
    ppermute x4, starting transfers between devices, shift(): return lax.ppermute(x, 'zh', [(i, (i + step) % n) for i in range(n)])  14.8 us
    all_gather x1, blocking collectives, shards(): weight_all = lax.all_gather(weight_all, 'x', axis=0, tiled=True)  11.7 us
    ppermute x4, starting transfers between devices, swap(): return lax.ppermute(x, 'core', [(0, 1), (1, 0)])  10.5 us
    all_to_all x1, starting transfers between devices, shards(): lax.all_to_all(term.reshape(dp_count, -1, width), DP, split_axis=0, conca...  10.4 us
  transfers between devices with their start and end apart: 13, of which 6 were waited for; matrix products, arithmetic and copies ran while one was open for 4% of the time, Pallas kernels for 7%

profile of v1, /device:TPU:1, one launch (start us, length us, event | category | flops | bytes accessed | tf_op | source)
XLA Modules:
  0.0 261.2 jit_solution(12447135673755959218)
XLA Ops:
  6.5 1.4 copy.10
  7.9 0.2 copy.11
  8.2 0.3 copy.12
  8.4 0.2 copy.13
  8.7 0.3 copy-done.2
  9.0 0.3 copy.14
  9.2 0.2 copy.15
  9.5 1.3 pad_maximum_fusion
  10.8 11.9 %all-to-all-start = ((bf16[8,3,128,256]{3,2,1,0:T(8,128)(2,1)}), bf16[8,3,128,256]{3,2,1,0:T(8,128)(2,1)S(1)}, u32[]{:S(2)}, u32[]{:S(2)}) async-start(bf16[8,3,128,256]{3,2,1,0:T(8,128)(2,1)} %pad_maximum_fusion), calls=%async_computation | async-start | bytes 3145728 | tf_op jit(solution)/shard_map/all_to_all | solution.py:167
  22.7 0.3 copy.16
  23.0 0.2 copy.17
  23.2 1.3 copy.18
  24.5 0.2 copy.19
  24.7 1.3 copy.20
  26.1 1.0 copy.21
  27.1 2.4 pad_maximum_fusion.1
  29.4 22.4 %all-to-all-done.q_ref.k_ref.v_ref = bf16[8,3,128,256]{3,2,1,0:T(8,128)(2,1)S(1)} async-done(((bf16[8,3,128,256]{3,2,1,0:T(8,128)(2,1)}), bf16[8,3,128,256]{3,2,1,0:T(8,128)(2,1)S(1)}, u32[]{:S(2)}, u32[]{:S(2)}) %all-to-all-start) | async-done | bytes 1572896 | tf_op jit(solution)/shard_map/all_to_all | solution.py:167
  51.9 15.1 %all-to-all-start.1 = ((bf16[8,3,128,256]{3,2,1,0:T(8,128)(2,1)}), bf16[8,3,128,256]{3,2,1,0:T(8,128)(2,1)S(1)}, u32[]{:S(2)}, u32[]{:S(2)}) async-start(bf16[8,3,128,256]{3,2,1,0:T(8,128)(2,1)} %pad_maximum_fusion.1), calls=%async_computation.1 | async-start | bytes 3145728 | tf_op jit(solution)/shard_map/all_to_all | solution.py:167
  67.0 8.1 %attend.1.refs_0_ = bf16[256,1024]{1,0:T(8,128)(2,1)} custom-call(bf16[8,3,128,256]{3,2,1,0:T(8,128)(2,1)S(1)} %all-to-all-done.q_ref.k_ref.v_ref, bf16[8,3,128,256]{3,2,1,0:T(8,128)(2,1)S(1)} %all-to-all-done.q_ref.k_ref.v_ref, bf16[8,3,128,256]{3,2,1,0:T(8,128)(2,1)S(1)} %all-to-all-done.q_ref.k_ref.v_ref), custom_call_target="tpu_custom_call" | custom-call | flops 2147483648 | bytes 8388608 | tf_op jit(solution)/shard_map/attend/pallas_call | solution.py:70
  75.1 4.2 %collective-permute-start = (bf16[256,1024]{1,0:T(8,128)(2,1)}, bf16[256,1024]{1,0:T(8,128)(2,1)}, u32[]{:S(2)}, u32[]{:S(2)}) collective-permute-start(bf16[256,1024]{1,0:T(8,128)(2,1)} %attend.1.refs_0_), channel_id=1, source_target_pairs={{0,2},{2,4},{4,6},{6,0},{1,3},{3,5},{5,7},{7,1},{8,10},{10,12},{12... | collective-permute-start | bytes 1572872 | tf_op jit(solution)/shard_map/ppermute | solution.py:142
  79.3 3.2 %collective-permute-start.1 = (bf16[256,1024]{1,0:T(8,128)(2,1)}, bf16[256,1024]{1,0:T(8,128)(2,1)}, u32[]{:S(2)}, u32[]{:S(2)}) collective-permute-start(bf16[256,1024]{1,0:T(8,128)(2,1)} %attend.1.refs_0_), channel_id=1, source_target_pairs={{0,6},{2,0},{4,2},{6,4},{1,7},{3,1},{5,3},{7,5},{8,14},{10,8},{12,... | collective-permute-start | bytes 1572872 | tf_op jit(solution)/shard_map/ppermute | solution.py:142
  82.5 45.3 %collective-permute-done.refs_1_ = bf16[256,1024]{1,0:T(8,128)(2,1)} collective-permute-done((bf16[256,1024]{1,0:T(8,128)(2,1)}, bf16[256,1024]{1,0:T(8,128)(2,1)}, u32[]{:S(2)}, u32[]{:S(2)}) %collective-permute-start) | collective-permute-done | bytes 524320 | tf_op jit(solution)/shard_map/ppermute | solution.py:142
  127.8 1.0 slice.8
  128.8 1.9 collective-permute-start.2
  130.7 1.0 slice.9
  131.7 5.5 %collective-permute-start.3 = (bf16[128,1024]{1,0:T(8,128)(2,1)S(1)}, bf16[128,1024]{1,0:T(8,128)(2,1)S(1)}, u32[]{:S(2)}, u32[]{:S(2)}) collective-permute-start(bf16[128,1024]{1,0:T(8,128)(2,1)S(1)} %slice.9), channel_id=1, source_target_pairs={{0,6},{2,0},{4,2},{6,4},{1,7},{3,1},{5,3},{7,5},{8,14},{10,8},{12,... | collective-permute-start | bytes 786440 | tf_op jit(solution)/shard_map/ppermute | solution.py:142
  137.2 3.3 %collective-permute-start.4 = (bf16[256,1024]{1,0:T(8,128)(2,1)}, bf16[256,1024]{1,0:T(8,128)(2,1)}, u32[]{:S(2)}, u32[]{:S(2)}) collective-permute-start(bf16[256,1024]{1,0:T(8,128)(2,1)} %attend.1.refs_0_), channel_id=1, source_target_pairs={{0,1},{1,0},{2,3},{3,2},{4,5},{5,4},{6,7},{7,6},{8,9},{9,8},{10,11... | collective-permute-start | bytes 1572872 | tf_op jit(solution)/shard_map/ppermute | solution.py:146
  140.5 1.9 collective-permute-start.6
  142.5 2.4 collective-permute-start.5
  144.9 0.7 constant_dynamic-update-slice_fusion.1
  145.6 0.4 collective-permute-done.3
  146.0 0.7 constant_dynamic-update-slice_fusion.refs_3_
  146.7 2.8 %collective-permute-start.7 = (bf16[256,1024]{1,0:T(8,128)(2,1)}, bf16[256,1024]{1,0:T(8,128)(2,1)}, u32[]{:S(2)}, u32[]{:S(2)}) collective-permute-start(bf16[256,1024]{1,0:T(8,128)(2,1)} %constant_dynamic-update-slice_fusion.refs_3_), channel_id=1, source_target_pairs={{0,1},{1,0},{2,3},{3,2},{4,5},{5,4},{6,7},{7,6},{8,9},{9,8},{10,11... | collective-permute-start | bytes 1572872 | tf_op jit(solution)/shard_map/ppermute | solution.py:146
  150.9 0.1 stack.59.place_ref
  151.0 10.4 %tangent.1.refs_8_ = bf16[1024,256]{1,0:T(8,128)(2,1)S(1)} custom-call(f32[1]{0:T(128)S(6)} %copy.23.coef_ref, bf16[8,3,128,256]{3,2,1,0:T(8,128)(2,1)S(1)} %all-to-all-done.q_ref.k_ref.v_ref, bf16[8,3,128,256]{3,2,1,0:T(8,128)(2,1)S(1)} %all-to-all-done.q_ref.k_ref.v_ref, bf16[8,3,128,256]{3,2,1,0:T(8,128)(2,1)S(1)} %all-to-all-done.q_ref.k_ref.v_ref, ...), custom_call_target="tpu_custom_call" | custom-call | flops 3758096384 | bytes 8388608 | tf_op jit(solution)/shard_map/tangent/pallas_call | solution.py:87
  161.4 4.8 %gram.1 = f32[8,256,256]{2,1,0:T(8,128)} custom-call(f32[1]{0:T(128)S(6)} %copy.24.weight_ref, s32[8]{0:T(128)S(1)} %stack.59.place_ref, bf16[256,1024]{1,0:T(8,128)(2,1)} %attend.1.refs_0_, bf16[256,1024]{1,0:T(8,128)(2,1)} %collective-permute-done.refs_1_, bf16[256,1024]{1,0:T(8,128)(2,1)} %collective-permute-done.1.refs_2_, ...), custom_call_target="tpu_custom_call" | custom-call | tf_op jit(solution)/shard_map/gram/pallas_call | solution.py:112
  166.2 10.4 %all-to-all-start.2 = ((f32[64,32,256]{2,1,0:T(8,128)}), f32[64,32,256]{2,1,0:T(8,128)S(1)}, u32[]{:S(2)}, u32[]{:S(2)}) async-start(f32[64,32,256]{2,1,0:T(8,128)} %bitcast.26), calls=%async_computation.2 | async-start | bytes 4194304 | tf_op jit(solution)/shard_map/all_to_all | solution.py:190
  176.7 0.0 all-gather.2.cloned.1.call-start
  176.7 6.0 %all_gather.9 = bf16[64,384]{1,0:T(8,128)(2,1)S(1)} all-gather(bf16[32,384]{1,0:T(8,128)(2,1)S(1)} %copy-done.4), channel_id=1, replica_groups=mesh['y'=8,'x'=4,'zl'=2,'zh'=4,'core'=2] {'zl'}, dimensions={0}, use_global_device_ids=true | all-gather | bytes 73728 | tf_op jit(solution)/shard_map/all_gather | solution.py:181
  182.7 11.7 %all_gather.10 = bf16[256,384]{1,0:T(8,128)(2,1)} all-gather(bf16[64,384]{1,0:T(8,128)(2,1)S(1)} %all_gather.9), channel_id=1, replica_groups=mesh['y'=8,'x'=4,'zl'=2,'zh'=4,'core'=2] {'x'}, dimensions={0}, use_global_device_ids=true | all-gather | bytes 245760 | tf_op jit(solution)/shard_map/all_gather | solution.py:182
  194.4 34.9 %all-to-all-done.2 = f32[64,32,256]{2,1,0:T(8,128)S(1)} async-done(((f32[64,32,256]{2,1,0:T(8,128)}), f32[64,32,256]{2,1,0:T(8,128)S(1)}, u32[]{:S(2)}, u32[]{:S(2)}) %all-to-all-start.2) | async-done | bytes 2097184 | tf_op jit(solution)/shard_map/all_to_all | solution.py:190
  229.4 0.1 reduce_sum.9
  229.5 0.7 broadcast_in_dim.2
  230.2 9.4 %all-to-all-start.3 = ((f32[8,32,256]{2,1,0:T(8,128)}), f32[8,32,256]{2,1,0:T(8,128)S(1)}, u32[]{:S(2)}, u32[]{:S(2)}) async-start(f32[8,32,256]{2,1,0:T(8,128)} %broadcast_in_dim.2), calls=%async_computation.3 | async-start | bytes 524288 | tf_op jit(solution)/shard_map/all_to_all | solution.py:194
  239.6 5.3 %all-gather.2.cloned.1.call-done = bf16[2048,384]{1,0:T(8,128)(2,1)} async-done(((bf16[256,384]{1,0:T(8,128)(2,1)}), bf16[2048,384]{1,0:T(8,128)(2,1)}) %all-gather.2.cloned.1.call-update) | async-done | bytes 1572880 | tf_op jit(solution)/shard_map/all_gather | solution.py:183
  244.9 6.9 %all-to-all-done.3.g_ref = f32[8,32,256]{2,1,0:T(8,128)S(1)} async-done(((f32[8,32,256]{2,1,0:T(8,128)}), f32[8,32,256]{2,1,0:T(8,128)S(1)}, u32[]{:S(2)}, u32[]{:S(2)}) %all-to-all-start.3) | async-done | bytes 262176 | tf_op jit(solution)/shard_map/all_to_all | solution.py:194
  251.8 1.4 copy-done
  253.2 1.2 finish.1
  (16 shorter events, 0.1 us)
Async XLA Ops:
  6.5 1.6 copy-start.1
  7.9 1.0 copy-start.2
  10.8 11.9 %copy-start.3 = (bf16[128,2048]{1,0:T(8,128)(2,1)S(1)}, bf16[128,2048]{1,0:T(8,128)(2,1)}, u32[]{:S(2)}) copy-start(bf16[128,2048]{1,0:T(8,128)(2,1)} %param.12) | copy-start | bytes 1572868
  10.8 41.1 %all-to-all-start = ((bf16[8,3,128,256]{3,2,1,0:T(8,128)(2,1)}), bf16[8,3,128,256]{3,2,1,0:T(8,128)(2,1)S(1)}, u32[]{:S(2)}, u32[]{:S(2)}) async-start(bf16[8,3,128,256]{3,2,1,0:T(8,128)(2,1)} %pad_maximum_fusion), calls=%async_computation | async-start | bytes 3145728 | tf_op jit(solution)/shard_map/all_to_all | solution.py:167
  51.9 99.1 %all-to-all-start.1 = ((bf16[8,3,128,256]{3,2,1,0:T(8,128)(2,1)}), bf16[8,3,128,256]{3,2,1,0:T(8,128)(2,1)S(1)}, u32[]{:S(2)}, u32[]{:S(2)}) async-start(bf16[8,3,128,256]{3,2,1,0:T(8,128)(2,1)} %pad_maximum_fusion.1), calls=%async_computation.1 | async-start | bytes 3145728 | tf_op jit(solution)/shard_map/all_to_all | solution.py:167
  75.1 52.7 %collective-permute-start = (bf16[256,1024]{1,0:T(8,128)(2,1)}, bf16[256,1024]{1,0:T(8,128)(2,1)}, u32[]{:S(2)}, u32[]{:S(2)}) collective-permute-start(bf16[256,1024]{1,0:T(8,128)(2,1)} %attend.1.refs_0_), channel_id=1, source_target_pairs={{0,2},{2,4},{4,6},{6,0},{1,3},{3,5},{5,7},{7,1},{8,10},{10,12},{12... | collective-permute-start | bytes 1572872 | tf_op jit(solution)/shard_map/ppermute | solution.py:142
  79.3 51.4 %collective-permute-start.1 = (bf16[256,1024]{1,0:T(8,128)(2,1)}, bf16[256,1024]{1,0:T(8,128)(2,1)}, u32[]{:S(2)}, u32[]{:S(2)}) collective-permute-start(bf16[256,1024]{1,0:T(8,128)(2,1)} %attend.1.refs_0_), channel_id=1, source_target_pairs={{0,6},{2,0},{4,2},{6,4},{1,7},{3,1},{5,3},{7,5},{8,14},{10,8},{12,... | collective-permute-start | bytes 1572872 | tf_op jit(solution)/shard_map/ppermute | solution.py:142
  128.8 16.1 %collective-permute-start.2 = (bf16[128,1024]{1,0:T(8,128)(2,1)S(1)}, bf16[128,1024]{1,0:T(8,128)(2,1)S(1)}, u32[]{:S(2)}, u32[]{:S(2)}) collective-permute-start(bf16[128,1024]{1,0:T(8,128)(2,1)S(1)} %slice.8), channel_id=1, source_target_pairs={{0,2},{2,4},{4,6},{6,0},{1,3},{3,5},{5,7},{7,1},{8,10},{10,12},{12... | collective-permute-start | bytes 786440 | tf_op jit(solution)/shard_map/ppermute | solution.py:142
  131.7 14.3 %collective-permute-start.3 = (bf16[128,1024]{1,0:T(8,128)(2,1)S(1)}, bf16[128,1024]{1,0:T(8,128)(2,1)S(1)}, u32[]{:S(2)}, u32[]{:S(2)}) collective-permute-start(bf16[128,1024]{1,0:T(8,128)(2,1)S(1)} %slice.9), channel_id=1, source_target_pairs={{0,6},{2,0},{4,2},{6,4},{1,7},{3,1},{5,3},{7,5},{8,14},{10,8},{12,... | collective-permute-start | bytes 786440 | tf_op jit(solution)/shard_map/ppermute | solution.py:142
  137.2 24.2 %collective-permute-start.4 = (bf16[256,1024]{1,0:T(8,128)(2,1)}, bf16[256,1024]{1,0:T(8,128)(2,1)}, u32[]{:S(2)}, u32[]{:S(2)}) collective-permute-start(bf16[256,1024]{1,0:T(8,128)(2,1)} %attend.1.refs_0_), channel_id=1, source_target_pairs={{0,1},{1,0},{2,3},{3,2},{4,5},{5,4},{6,7},{7,6},{8,9},{9,8},{10,11... | collective-permute-start | bytes 1572872 | tf_op jit(solution)/shard_map/ppermute | solution.py:146
  140.5 20.9 %collective-permute-start.6 = (bf16[256,1024]{1,0:T(8,128)(2,1)}, bf16[256,1024]{1,0:T(8,128)(2,1)}, u32[]{:S(2)}, u32[]{:S(2)}) collective-permute-start(bf16[256,1024]{1,0:T(8,128)(2,1)} %collective-permute-done.1.refs_2_), channel_id=1, source_target_pairs={{0,1},{1,0},{2,3},{3,2},{4,5},{5,4},{6,7},{7,6},{8,9},{9,8},{10,11... | collective-permute-start | bytes 1572872 | tf_op jit(solution)/shard_map/ppermute | solution.py:146
  142.5 19.0 %collective-permute-start.5 = (bf16[256,1024]{1,0:T(8,128)(2,1)}, bf16[256,1024]{1,0:T(8,128)(2,1)}, u32[]{:S(2)}, u32[]{:S(2)}) collective-permute-start(bf16[256,1024]{1,0:T(8,128)(2,1)} %collective-permute-done.refs_1_), channel_id=1, source_target_pairs={{0,1},{1,0},{2,3},{3,2},{4,5},{5,4},{6,7},{7,6},{8,9},{9,8},{10,11... | collective-permute-start | bytes 1572872 | tf_op jit(solution)/shard_map/ppermute | solution.py:146
  146.7 14.7 %collective-permute-start.7 = (bf16[256,1024]{1,0:T(8,128)(2,1)}, bf16[256,1024]{1,0:T(8,128)(2,1)}, u32[]{:S(2)}, u32[]{:S(2)}) collective-permute-start(bf16[256,1024]{1,0:T(8,128)(2,1)} %constant_dynamic-update-slice_fusion.refs_3_), channel_id=1, source_target_pairs={{0,1},{1,0},{2,3},{3,2},{4,5},{5,4},{6,7},{7,6},{8,9},{9,8},{10,11... | collective-permute-start | bytes 1572872 | tf_op jit(solution)/shard_map/ppermute | solution.py:146
  166.2 10.5 %copy-start.4 = (bf16[32,384]{1,0:T(8,128)(2,1)S(1)}, bf16[32,384]{1,0:T(8,128)(2,1)}, u32[]{:S(2)}) copy-start(bf16[32,384]{1,0:T(8,128)(2,1)} %param.15) | copy-start | bytes 73732
  166.2 63.1 %all-to-all-start.2 = ((f32[64,32,256]{2,1,0:T(8,128)}), f32[64,32,256]{2,1,0:T(8,128)S(1)}, u32[]{:S(2)}, u32[]{:S(2)}) async-start(f32[64,32,256]{2,1,0:T(8,128)} %bitcast.26), calls=%async_computation.2 | async-start | bytes 4194304 | tf_op jit(solution)/shard_map/all_to_all | solution.py:190
  176.7 68.2 %all-gather.2.cloned.1.call-start = ((), (), s32[]{:S(2)}) async-start(), calls=%async_computation.4 | async-start | bytes 1769472 | tf_op jit(solution)/shard_map/all_gather | solution.py:183
  230.2 21.5 %all-to-all-start.3 = ((f32[8,32,256]{2,1,0:T(8,128)}), f32[8,32,256]{2,1,0:T(8,128)S(1)}, u32[]{:S(2)}, u32[]{:S(2)}) async-start(f32[8,32,256]{2,1,0:T(8,128)} %broadcast_in_dim.2), calls=%async_computation.3 | async-start | bytes 524288 | tf_op jit(solution)/shard_map/all_to_all | solution.py:194
  251.8 1.4 copy-start
Sparse Core Ops, SparseCore 0:
  194.6 50.2 all-gather.1

commit v2 on v1

v2 whole, which is shorter than its diff:
```python
import functools

import jax
import jax.numpy as jnp
from jax import lax
from jax.experimental import pallas as pl
from jax.experimental.pallas import tpu as pltpu
from jax.sharding import Mesh
from jax.sharding import PartitionSpec as P

HEAD = 128
LOSS_SCALE = 64.0
ROWS = 256
HALVES = 2
STEPS = (0, 3, 1, 2)
SEQ = ("zh", "core")
NEAR = ("x", "zl")
DP = ("y", "x", "zl")
NT = (((1,), (1,)), ((), ()))


def dot(a, b):
    return jnp.dot(a, b, preferred_element_type=jnp.float32)


def dot_nt(a, b):
    return lax.dot_general(a, b, NT, preferred_element_type=jnp.float32)


def flat(ref):
    return ref[...].reshape(-1, HEAD)


def probs_of(q, k, scale):
    scores = dot_nt(q, k) * scale
    expo = jnp.exp(scores - jnp.max(scores, axis=-1, keepdims=True))
    return expo / jnp.sum(expo, axis=-1, keepdims=True)


def forward_kernel(scale, q_ref, k_ref, v_ref, at_ref):
    low = probs_of(flat(q_ref), flat(k_ref), scale).astype(jnp.bfloat16)
    at_ref[...] = dot(low, flat(v_ref)).T.astype(jnp.bfloat16)


def tangent_kernel(
    scale, coef_ref, q_ref, k_ref, v_ref, dq_ref, dk_ref, dv_ref, mixed_ref
):
    q, k, v = flat(q_ref), flat(k_ref), flat(v_ref)
    probs = probs_of(q, k, scale)
    low = probs.astype(jnp.bfloat16)
    left = jnp.concatenate([flat(dq_ref), q], axis=1)
    right = jnp.concatenate([k, flat(dk_ref)], axis=1)
    d_scores = dot_nt(left, right) * scale
    shift = jnp.sum(probs * d_scores, axis=-1, keepdims=True)
    d_low = (probs * (d_scores - shift)).astype(jnp.bfloat16)
    tangent = (dot(d_low, v) + dot(low, flat(dv_ref))).astype(jnp.bfloat16)
    attended = dot(low, v).astype(jnp.bfloat16)
    mixed_ref[...] = (
        attended.astype(jnp.float32) + coef_ref[0] * tangent.astype(jnp.float32)
    ).astype(jnp.bfloat16)


def attention_specs(seq_count, tokens, arrays, head=0):
    per = ROWS // tokens
    query = lambda n: pl.BlockSpec((per, 1, tokens, HEAD), lambda h, i: (i, n, 0, h + head))
    whole = lambda n: pl.BlockSpec(
        (seq_count, 1, tokens, HEAD), lambda h, i: (0, n, 0, h + head)
    )
    return [query(0), whole(1), whole(2)] * arrays


def attend(qkv, head, scale):
    seq_count, _, tokens, _ = qkv.shape
    length = seq_count * tokens
    return pl.pallas_call(
        functools.partial(forward_kernel, scale),
        grid=(1, length // ROWS),
        in_specs=attention_specs(seq_count, tokens, 1, head),
        out_specs=pl.BlockSpec((HEAD, ROWS), lambda h, i: (h, i)),
        out_shape=jax.ShapeDtypeStruct((HEAD, length), jnp.bfloat16),
        compiler_params=pltpu.CompilerParams(vmem_limit_bytes=8 << 20),
        cost_estimate=pl.CostEstimate(
            flops=4 * length * length * HEAD, bytes_accessed=2 << 20, transcendentals=length * length
        ),
        name="attend",
    )(qkv, qkv, qkv)


def attend_tangent(coef, qkv, d_qkv, scale):
    seq_count, _, tokens, width = qkv.shape
    length = seq_count * tokens
    return pl.pallas_call(
        functools.partial(tangent_kernel, scale),
        grid=(width // HEAD, length // ROWS),
        in_specs=[pl.BlockSpec(memory_space=pltpu.SMEM)] + attention_specs(seq_count, tokens, 2),
        out_specs=pl.BlockSpec((ROWS, HEAD), lambda h, i: (i, h)),
        out_shape=jax.ShapeDtypeStruct((length, width), jnp.bfloat16),
        compiler_params=pltpu.CompilerParams(vmem_limit_bytes=12 << 20),
        cost_estimate=pl.CostEstimate(
            flops=14 * length * length * width, bytes_accessed=8 << 20, transcendentals=length * length * 2
        ),
        name="tangent",
    )(coef, qkv, qkv, qkv, d_qkv, d_qkv, d_qkv)


def gram_kernel(weight_ref, at_ref, *refs):
    blocks, (own, other), out_ref = refs[: 4 * HALVES], refs[4 * HALVES : -2], refs[-1]
    near, depth, cols = out_ref.shape
    zh, core = at_ref[0], at_ref[1]
    part = blocks[0].shape[0] * HALVES // near
    span = near // HALVES
    peak = jnp.zeros((1, 1), jnp.float32)
    for n, step in enumerate(STEPS):
        chip = lax.rem(zh + step, 4)
        for half in range(HALVES):
            left = blocks[n * HALVES + half][...]
            for mixed_ref, side in ((own, core), (other, 1 - core)):
                block = weight_ref[0] * dot(left, mixed_ref[...])
                start = pl.multiple_of((chip * 2 + side) * part, part)
                out_ref[half * span : (half + 1) * span, pl.ds(start, part)] = block.reshape(
                    span, part, cols
                )
                peak = jnp.maximum(peak, jnp.max(jnp.abs(block), keepdims=True))
    out_ref[:, depth - 8 :] = jnp.broadcast_to(peak, (near, 8, cols))


def gram(weight, blocks, mixed, pieces, after):
    rows, cols = blocks[0].shape[0], mixed[0].shape[1]
    depth = 2 * len(blocks) * rows // pieces + 8
    at = jnp.stack([lax.axis_index("zh"), lax.axis_index("core")]).astype(jnp.int32)
    smem = pl.BlockSpec(memory_space=pltpu.SMEM)
    vmem = pl.BlockSpec(memory_space=pltpu.VMEM)
    return pl.pallas_call(
        gram_kernel,
        in_specs=[smem, smem] + [vmem] * (len(blocks) + 2) + [pl.BlockSpec(memory_space=pl.ANY)],
        out_specs=vmem,
        out_shape=jax.ShapeDtypeStruct((pieces, depth, cols), jnp.float32),
        compiler_params=pltpu.CompilerParams(vmem_limit_bytes=12 << 20),
        name="gram",
    )(weight, at, *blocks, *mixed, after)


def finish_kernel(factor, g_ref, w_ref, out_ref):
    total = jnp.zeros(out_ref.shape, jnp.float32)
    for n in range(g_ref.shape[0]):
        high = g_ref[n].astype(jnp.bfloat16)
        rest = (g_ref[n] - high.astype(jnp.float32)).astype(jnp.bfloat16)
        total = total + dot(high, w_ref[n]) + dot(rest, w_ref[n])
    out_ref[...] = total * factor


def finish(g, w, factor):
    return pl.pallas_call(
        functools.partial(finish_kernel, factor),
        out_shape=jax.ShapeDtypeStruct((g.shape[1], w.shape[2]), jnp.float32),
        compiler_params=pltpu.CompilerParams(vmem_limit_bytes=8 << 20),
        name="finish",
    )(g, w)


def shift(x, step):
    n = lax.axis_size("zh")
    return lax.ppermute(x, "zh", [(i, (i + step) % n) for i in range(n)])


def swap(x):
    return lax.ppermute(x, "core", [(0, 1), (1, 0)])


def neighbours(x):
    return shift(x, 1), shift(x, -1)


def settle(x):
    pairs = []
    for y in range(0, lax.axis_size("y"), 2):
        low, high = y * 2 + 1, (y + 1) * 2
        pairs += [(low, high), (high, low)]
    moved = lax.ppermute(x, ("y", "core"), pairs)
    stays = lax.axis_index("y") % 2 == lax.axis_index("core")
    return jnp.where(stays, x, moved)


def exchange(x, axes):
    return lax.all_to_all(x, axes, split_axis=0, concat_axis=0, tiled=True)


def by_heads(arrays, seq_count):
    return jnp.stack(
        [x.reshape(x.shape[0], seq_count, -1).transpose(1, 0, 2) for x in arrays], axis=1
    )


def reduce_near(term):
    count = term.shape[1] - 8
    power = jnp.ceil(jnp.log2(jnp.maximum(term[0, count, 0], 1e-30))) - 15.0
    row = lax.broadcasted_iota(jnp.int32, term.shape, 1)
    held = jnp.where(row < count, term * jnp.exp2(-power), power).astype(jnp.float16)
    parts = exchange(held, NEAR).astype(jnp.float32)
    return jnp.sum(parts[:, :count] * jnp.exp2(parts[:, count : count + 1, :1]), axis=0)


def shards(
    queries, keys, values, d_queries, d_keys, d_values, out_weight, tangent_coef, loss_weight
):
    seq_count = lax.axis_size(SEQ)
    dp_count = lax.axis_size(DP)
    length = queries.shape[0] * seq_count
    scale = 1.0 / HEAD**0.5

    qkv = by_heads((queries, keys, values), seq_count)
    d_qkv = by_heads((d_queries, d_keys, d_values), seq_count)
    pair = lax.all_gather(out_weight, "zl", axis=0, tiled=True)
    qkv, pair = lax.optimization_barrier((qkv, pair))
    weight_part = lax.all_gather(pair, "x", axis=0, tiled=True)
    d_qkv, weight_part = lax.optimization_barrier((d_qkv, weight_part))
    weight_all = lax.all_gather(weight_part, "y", axis=0, tiled=True)
    qkv, d_qkv = exchange(qkv, SEQ), exchange(d_qkv, SEQ)
    first, second = attend(qkv, 0, scale), attend(qkv, 1, scale)
    before_first, after_first = neighbours(first)
    before_second, after_second = neighbours(second)
    mixed = attend_tangent(tangent_coef, qkv, d_qkv, scale)
    before_first, before_second, after_first, after_second, mixed = lax.optimization_barrier(
        (before_first, before_second, after_first, after_second, mixed)
    )
    mixed_pair = (mixed, swap(mixed))
    far_first, far_second = shift(before_first, 1), shift(after_second, -1)
    blocks = (
        first, second, before_first, before_second,
        after_first, after_second, far_first, far_second,
    )
    term = gram(loss_weight, blocks, mixed_pair, lax.axis_size(NEAR), weight_all[:16, :HEAD])
    summed = reduce_near(term).reshape(lax.axis_size("y"), -1, mixed.shape[1])
    summed = settle(jnp.sum(exchange(summed, "y"), axis=0))
    rows = exchange(jnp.broadcast_to(summed[None], (seq_count,) + summed.shape), SEQ)
    total_tokens = length * dp_count
    return finish(
        rows, weight_all.reshape(seq_count, mixed.shape[1], -1), LOSS_SCALE / total_tokens**0.5
    )


def solution(mesh):
    split = Mesh(mesh.devices.reshape(8, 4, 2, 4, 2), DP + SEQ)
    tokens = P(DP + SEQ, None)
    placed = (tokens,) * 6 + (P(DP, SEQ), P(DP), P(DP))
    return jax.shard_map(
        shards, mesh=split, in_specs=placed, out_specs=P(DP, SEQ), check_vma=False
    )
```

time: 262 us -> 228 us (0.87)
  waiting for transfers between devices: 115 us -> 51.3 us
  blocking collectives: 17.7 us -> 64.2 us
  starting transfers between devices: 72.2 us -> 57.7 us
  local copies, waits for them, and re-layouts: 12.8 us -> 9.6 us
    all_to_all x0 -> x3, blocking collectives: none -> 48.6 us  [exchange(): return lax.all_to_all(x, axes, split_axis=0, concat_axis=0, tiled=True)]
    all_to_all x4 -> x2, waiting for transfers between devices: 64.3 us -> 33.3 us  [exchange(): return lax.all_to_all(x, axes, split_axis=0, concat_axis=0, tiled=True)]
    ppermute x4 -> x6, waiting for transfers between devices: 45.7 us -> 15.7 us  [shift(): return lax.ppermute(x, 'zh', [(i, (i + step) % n) for i in range(n)])]
    all_to_all x4 -> x2, starting transfers between devices: 46.9 us -> 26.8 us  [exchange(): return lax.all_to_all(x, axes, split_axis=0, concat_axis=0, tiled=True)]
    ppermute x4 -> x1, starting transfers between devices: 10.5 us -> 2.77 us  [swap(): return lax.ppermute(x, 'core', [(0, 1), (1, 0)])]
    ppermute x4 -> x6, starting transfers between devices: 14.8 us -> 22.2 us  [shift(): return lax.ppermute(x, 'zh', [(i, (i + step) % n) for i in range(n)])]
    ppermute x0 -> x1, starting transfers between devices: none -> 5.95 us  [settle(): moved = lax.ppermute(x, ('y', 'core'), pairs)]
    all_gather x1, waiting for transfers between devices: 5.28 us -> 0.01 us  [shards(): weight_all = lax.all_gather(weight_part, 'y', axis=0, tiled=True)]
  transfers between devices with their start and end apart: 13 -> 11, of which waited for: 6 -> 6; matrix products, arithmetic and copies ran while one was open for 4% -> 3% of each run, Pallas kernels for 7% -> 8%
where the time goes in v2:
time: 228 us; the launch traced here: 226 us
  blocking collectives  64.2 us (28%)
  starting transfers between devices  57.7 us (25%)
  waiting for transfers between devices  51.3 us (22%)
  Pallas kernels  23.2 us (10%)
  between operations  15.6 us (7%)
  local copies, waits for them, and re-layouts  9.6 us (4%)
  other arithmetic  4.62 us (2%)
    all_to_all x3, blocking collectives, exchange(): return lax.all_to_all(x, axes, split_axis=0, concat_axis=0, tiled=True)  48.6 us
    all_to_all x2, waiting for transfers between devices, exchange(): return lax.all_to_all(x, axes, split_axis=0, concat_axis=0, tiled=True)  33.3 us
    all_to_all x2, starting transfers between devices, exchange(): return lax.all_to_all(x, axes, split_axis=0, concat_axis=0, tiled=True)  26.8 us
    ppermute x6, starting transfers between devices, shift(): return lax.ppermute(x, 'zh', [(i, (i + step) % n) for i in range(n)])  22.2 us
    ppermute x6, waiting for transfers between devices, shift(): return lax.ppermute(x, 'zh', [(i, (i + step) % n) for i in range(n)])  15.7 us
    pallas_call x1, Pallas kernels, attend_tangent(): pl.pallas_call(functools.partial(tangent_kernel, scale), grid=(width // H...  11 us
    all_gather x1, blocking collectives, shards(): weight_part = lax.all_gather(pair, 'x', axis=0, tiled=True)  10.9 us
    pallas_call x2, Pallas kernels, attend(): pl.pallas_call(functools.partial(forward_kernel, scale), grid=(1, length...  8.18 us
  transfers between devices with their start and end apart: 11, of which 6 were waited for; matrix products, arithmetic and copies ran while one was open for 3% of the time, Pallas kernels for 8%

profile of v2, /device:TPU:1, one launch (start us, length us, event | category | flops | bytes accessed | tf_op | source)
XLA Modules:
  0.0 226.2 jit_solution(9158823873357480166)
XLA Ops:
  6.5 1.4 copy.26
  7.9 0.2 copy.27
  8.2 0.3 copy.22
  8.7 0.3 copy-done.4
  9.0 0.3 copy.24
  9.2 0.2 copy.25
  9.5 4.8 %all_gather.9 = bf16[64,384]{1,0:T(8,128)(2,1)S(1)} all-gather(bf16[32,384]{1,0:T(8,128)(2,1)S(1)} %copy-done.7), channel_id=1, replica_groups=mesh['y'=8,'x'=4,'zl'=2,'zh'=4,'core'=2] {'zl'}, dimensions={0}, use_global_device_ids=true | all-gather | bytes 73728 | tf_op jit(solution)/shard_map/all_gather | solution.py:213
  14.3 1.3 pad_maximum_fusion
  15.6 11.7 %all-to-all-start = ((bf16[8,3,128,256]{3,2,1,0:T(8,128)(2,1)}), bf16[8,3,128,256]{3,2,1,0:T(8,128)(2,1)S(1)}, u32[]{:S(2)}, u32[]{:S(2)}) async-start(bf16[8,3,128,256]{3,2,1,0:T(8,128)(2,1)} %pad_maximum_fusion), calls=%async_computation | async-start | bytes 3145728 | tf_op jit(solution)/shard_map/all_to_all | solution.py:185
  27.3 0.3 copy.28
  27.5 0.2 copy.29
  27.8 0.5 copy-done.6
  28.3 0.3 copy.30
  28.6 0.2 copy.31
  28.8 1.3 copy.32
  30.1 1.0 copy.33
  31.1 10.9 %all_gather.10 = bf16[256,384]{1,0:T(8,128)(2,1)} all-gather(bf16[64,384]{1,0:T(8,128)(2,1)S(1)} %all_gather.9), channel_id=1, replica_groups=mesh['y'=8,'x'=4,'zl'=2,'zh'=4,'core'=2] {'x'}, dimensions={0}, use_global_device_ids=true | all-gather | bytes 245760 | tf_op jit(solution)/shard_map/all_gather | solution.py:215
  42.0 2.3 %pad_maximum_fusion.1 = bf16[8,3,128,256]{3,2,1,0:T(8,128)(2,1)} fusion(bf16[8,1,128,256]{3,2,1,0:T(8,128)(2,1)} %bitcast.39, bf16[8,1,128,256]{3,2,1,0:T(8,128)(2,1)S(1)} %bitcast.37, bf16[8,1,128,256]{3,2,1,0:T(8,128)(2,1)S(1)} %bitcast.36), kind=kLoop, calls=%fused_computation.4 | loop fusion | flops 1572864 | bytes 3145728 | tf_op jit(solution)/shard_map/stack | solution.py:189
  44.4 12.1 %all-to-all-done.q_ref.k_ref.v_ref = bf16[8,3,128,256]{3,2,1,0:T(8,128)(2,1)S(1)} async-done(((bf16[8,3,128,256]{3,2,1,0:T(8,128)(2,1)}), bf16[8,3,128,256]{3,2,1,0:T(8,128)(2,1)S(1)}, u32[]{:S(2)}, u32[]{:S(2)}) %all-to-all-start) | async-done | bytes 1572896 | tf_op jit(solution)/shard_map/all_to_all | solution.py:185
  56.4 15.1 %all-to-all-start.1 = ((bf16[8,3,128,256]{3,2,1,0:T(8,128)(2,1)}), bf16[8,3,128,256]{3,2,1,0:T(8,128)(2,1)S(1)}, u32[]{:S(2)}, u32[]{:S(2)}) async-start(bf16[8,3,128,256]{3,2,1,0:T(8,128)(2,1)} %pad_maximum_fusion.1), calls=%async_computation.1 | async-start | bytes 3145728 | tf_op jit(solution)/shard_map/all_to_all | solution.py:185
  71.6 0.7 all-gather.2.cloned.1.call-update
  72.9 3.8 %attend.2.refs_0_ = bf16[128,1024]{1,0:T(8,128)(2,1)S(1)} custom-call(bf16[8,3,128,256]{3,2,1,0:T(8,128)(2,1)S(1)} %all-to-all-done.q_ref.k_ref.v_ref, bf16[8,3,128,256]{3,2,1,0:T(8,128)(2,1)S(1)} %all-to-all-done.q_ref.k_ref.v_ref, bf16[8,3,128,256]{3,2,1,0:T(8,128)(2,1)S(1)} %all-to-all-done.q_ref.k_ref.v_ref), custom_call_target="tpu_custom_call" | custom-call | flops 536870912 | bytes 2097152 | tf_op jit(solution)/shard_map/attend/pallas_call | solution.py:75
  76.7 4.2 %collective-permute-start = (bf16[128,1024]{1,0:T(8,128)(2,1)S(1)}, bf16[128,1024]{1,0:T(8,128)(2,1)}, u32[]{:S(2)}, u32[]{:S(2)}) collective-permute-start(bf16[128,1024]{1,0:T(8,128)(2,1)S(1)} %attend.2.refs_0_), channel_id=1, source_target_pairs={{0,2},{2,4},{4,6},{6,0},{1,3},{3,5},{5,7},{7,1},{8,10},{10,12},{12... | collective-permute-start | bytes 786440 | tf_op jit(solution)/shard_map/ppermute | solution.py:163
  81.0 3.2 %collective-permute-start.2 = (bf16[128,1024]{1,0:T(8,128)(2,1)S(1)}, bf16[128,1024]{1,0:T(8,128)(2,1)}, u32[]{:S(2)}, u32[]{:S(2)}) collective-permute-start(bf16[128,1024]{1,0:T(8,128)(2,1)S(1)} %attend.2.refs_0_), channel_id=1, source_target_pairs={{0,6},{2,0},{4,2},{6,4},{1,7},{3,1},{5,3},{7,5},{8,14},{10,8},{12,... | collective-permute-start | bytes 786440 | tf_op jit(solution)/shard_map/ppermute | solution.py:163
  84.2 4.4 %attend.3.refs_1_ = bf16[128,1024]{1,0:T(8,128)(2,1)} custom-call(bf16[8,3,128,256]{3,2,1,0:T(8,128)(2,1)S(1)} %all-to-all-done.q_ref.k_ref.v_ref, bf16[8,3,128,256]{3,2,1,0:T(8,128)(2,1)S(1)} %all-to-all-done.q_ref.k_ref.v_ref, bf16[8,3,128,256]{3,2,1,0:T(8,128)(2,1)S(1)} %all-to-all-done.q_ref.k_ref.v_ref), custom_call_target="tpu_custom_call" | custom-call | flops 536870912 | bytes 2097152 | tf_op jit(solution)/shard_map/attend/pallas_call | solution.py:75
  88.5 3.9 %collective-permute-start.1 = (bf16[128,1024]{1,0:T(8,128)(2,1)}, bf16[128,1024]{1,0:T(8,128)(2,1)}, u32[]{:S(2)}, u32[]{:S(2)}) collective-permute-start(bf16[128,1024]{1,0:T(8,128)(2,1)} %attend.3.refs_1_), channel_id=1, source_target_pairs={{0,2},{2,4},{4,6},{6,0},{1,3},{3,5},{5,7},{7,1},{8,10},{10,12},{12... | collective-permute-start | bytes 786440 | tf_op jit(solution)/shard_map/ppermute | solution.py:163
  92.5 3.5 %collective-permute-start.3 = (bf16[128,1024]{1,0:T(8,128)(2,1)}, bf16[128,1024]{1,0:T(8,128)(2,1)}, u32[]{:S(2)}, u32[]{:S(2)}) collective-permute-start(bf16[128,1024]{1,0:T(8,128)(2,1)} %attend.3.refs_1_), channel_id=1, source_target_pairs={{0,6},{2,0},{4,2},{6,4},{1,7},{3,1},{5,3},{7,5},{8,14},{10,8},{12,... | collective-permute-start | bytes 786440 | tf_op jit(solution)/shard_map/ppermute | solution.py:163
  95.9 21.2 %all-to-all-done.1.dq_ref.dk_ref.dv_ref = bf16[8,3,128,256]{3,2,1,0:T(8,128)(2,1)S(1)} async-done(((bf16[8,3,128,256]{3,2,1,0:T(8,128)(2,1)}), bf16[8,3,128,256]{3,2,1,0:T(8,128)(2,1)S(1)}, u32[]{:S(2)}, u32[]{:S(2)}) %all-to-all-start.1) | async-done | bytes 1572896 | tf_op jit(solution)/shard_map/all_to_all | solution.py:185
  117.1 11.0 %tangent.1.refs_8_ = bf16[1024,256]{1,0:T(8,128)(2,1)} custom-call(f32[1]{0:T(128)S(6)} %copy.34.coef_ref, bf16[8,3,128,256]{3,2,1,0:T(8,128)(2,1)S(1)} %all-to-all-done.q_ref.k_ref.v_ref, bf16[8,3,128,256]{3,2,1,0:T(8,128)(2,1)S(1)} %all-to-all-done.q_ref.k_ref.v_ref, bf16[8,3,128,256]{3,2,1,0:T(8,128)(2,1)S(1)} %all-to-all-done.q_ref.k_ref.v_ref, ...), custom_call_target="tpu_custom_call" | custom-call | flops 3758096384 | bytes 8388608 | tf_op jit(solution)/shard_map/tangent/pallas_call | solution.py:92
  128.2 4.2 %collective-permute-done.1.refs_3_ = bf16[128,1024]{1,0:T(8,128)(2,1)} collective-permute-done((bf16[128,1024]{1,0:T(8,128)(2,1)}, bf16[128,1024]{1,0:T(8,128)(2,1)}, u32[]{:S(2)}, u32[]{:S(2)}) %collective-permute-start.1) | collective-permute-done | bytes 262176 | tf_op jit(solution)/shard_map/ppermute | solution.py:163
  132.4 2.8 %collective-permute-start.6 = (bf16[1024,256]{1,0:T(8,128)(2,1)}, bf16[1024,256]{1,0:T(8,128)(2,1)S(1)}, u32[]{:S(2)}, u32[]{:S(2)}) collective-permute-start(bf16[1024,256]{1,0:T(8,128)(2,1)} %tangent.1.refs_8_), channel_id=1, source_target_pairs={{0,1},{1,0},{2,3},{3,2},{4,5},{5,4},{6,7},{7,6},{8,9},{9,8},{10,11... | collective-permute-start | bytes 1572872 | tf_op jit(solution)/shard_map/ppermute | solution.py:167
  135.2 3.9 %collective-permute-start.4 = (bf16[128,1024]{1,0:T(8,128)(2,1)}, bf16[128,1024]{1,0:T(8,128)(2,1)S(1)}, u32[]{:S(2)}, u32[]{:S(2)}) collective-permute-start(bf16[128,1024]{1,0:T(8,128)(2,1)} %collective-permute-done.refs_2_), channel_id=1, source_target_pairs={{0,2},{2,4},{4,6},{6,0},{1,3},{3,5},{5,7},{7,1},{8,10},{10,12},{12... | collective-permute-start | bytes 786440 | tf_op jit(solution)/shard_map/ppermute | solution.py:163
  139.1 3.5 %collective-permute-start.5 = (bf16[128,1024]{1,0:T(8,128)(2,1)}, bf16[128,1024]{1,0:T(8,128)(2,1)S(1)}, u32[]{:S(2)}, u32[]{:S(2)}) collective-permute-start(bf16[128,1024]{1,0:T(8,128)(2,1)} %collective-permute-done.3.refs_5_), channel_id=1, source_target_pairs={{0,6},{2,0},{4,2},{6,4},{1,7},{3,1},{5,3},{7,5},{8,14},{10,8},{12,... | collective-permute-start | bytes 786440 | tf_op jit(solution)/shard_map/ppermute | solution.py:163
  143.3 0.7 slice.16.refs_10_
  144.0 6.9 %collective-permute-done.4.refs_6_ = bf16[128,1024]{1,0:T(8,128)(2,1)S(1)} collective-permute-done((bf16[128,1024]{1,0:T(8,128)(2,1)}, bf16[128,1024]{1,0:T(8,128)(2,1)S(1)}, u32[]{:S(2)}, u32[]{:S(2)}) %collective-permute-start.4) | collective-permute-done | bytes 262176 | tf_op jit(solution)/shard_map/ppermute | solution.py:163
  150.9 4.6 %collective-permute-done.5.refs_7_ = bf16[128,1024]{1,0:T(8,128)(2,1)S(1)} collective-permute-done((bf16[128,1024]{1,0:T(8,128)(2,1)}, bf16[128,1024]{1,0:T(8,128)(2,1)S(1)}, u32[]{:S(2)}, u32[]{:S(2)}) %collective-permute-start.5) | collective-permute-done | bytes 262176 | tf_op jit(solution)/shard_map/ppermute | solution.py:163
  155.5 0.7 copy-done.1
  156.2 0.9 copy-done.2
  157.2 2.8 %gram.1 = f32[8,264,256]{2,1,0:T(8,128)S(1)} custom-call(f32[1]{0:T(128)S(6)} %copy.35.weight_ref, s32[2]{0:T(128)S(1)} %pad_add_fusion.at_ref, bf16[128,1024]{1,0:T(8,128)(2,1)S(1)} %attend.2.refs_0_, bf16[128,1024]{1,0:T(8,128)(2,1)} %attend.3.refs_1_, bf16[128,1024]{1,0:T(8,128)(2,1)} %collective-permute-done.refs_2_, ...), custom_call_target="tpu_custom_call" | custom-call | tf_op jit(solution)/shard_map/gram/pallas_call | solution.py:133
  160.0 0.5 slice.17
  161.2 0.3 select_convert_fusion
  161.5 18.5 %all_to_all.25 = f16[8,264,256]{2,1,0:T(8,128)(2,1)S(1)} all-to-all(f16[8,264,256]{2,1,0:T(8,128)(2,1)S(1)} %select_convert_fusion), channel_id=1, replica_groups=mesh['y'=8,'x'=4,'zl'=2,'zh'=4,'core'=2] {'x','zl'}, dimensions={0} | all-to-all | bytes 2162688 | tf_op jit(solution)/shard_map/all_to_all | solution.py:185
  180.3 0.2 fusion
  180.5 16.2 %all_to_all.26 = f32[8,32,256]{2,1,0:T(8,128)S(1)} all-to-all(f32[8,32,256]{2,1,0:T(8,128)S(1)} %bitcast.42), channel_id=1, replica_groups=mesh['y'=8,'x'=4,'zl'=2,'zh'=4,'core'=2] {'y'}, dimensions={0} | all-to-all | bytes 524288 | tf_op jit(solution)/shard_map/all_to_all | solution.py:185
  196.7 6.0 %collective-permute-start.7 = (f32[32,256]{1,0:T(8,128)S(1)}, f32[32,256]{1,0:T(8,128)S(1)}, u32[]{:S(2)}, u32[]{:S(2)}) collective-permute-start(f32[32,256]{1,0:T(8,128)S(1)} %reduce_sum.19), channel_id=1, source_target_pairs={{1,64},{64,1},{129,192},{192,129},{257,320},{320,257},{385,448},{4... | collective-permute-start | bytes 98312 | tf_op jit(solution)/shard_map/ppermute | solution.py:179
  202.7 1.6 collective-permute-done.7
  204.3 13.9 %all_to_all.27.g_ref = f32[8,32,256]{2,1,0:T(8,128)S(1)} all-to-all(f32[8,32,256]{2,1,0:T(8,128)S(1)} %broadcast_in_dim.11), channel_id=1, replica_groups=mesh['y'=8,'x'=4,'zl'=2,'zh'=4,'core'=2] {'zh','core'}, dimensions={0} | all-to-all | bytes 524288 | tf_op jit(solution)/shard_map/all_to_all | solution.py:185
  218.2 1.2 finish.1
  (26 shorter events, 0.7 us)
Async XLA Ops:
  6.5 1.6 copy-start.3
  7.9 1.0 copy-start.4
  8.4 1.0 copy-start.7
  15.6 11.7 %copy-start.5 = (bf16[128,2048]{1,0:T(8,128)(2,1)S(1)}, bf16[128,2048]{1,0:T(8,128)(2,1)}, u32[]{:S(2)}) copy-start(bf16[128,2048]{1,0:T(8,128)(2,1)} %param.12) | copy-start | bytes 1572868
  15.6 40.8 %all-to-all-start = ((bf16[8,3,128,256]{3,2,1,0:T(8,128)(2,1)}), bf16[8,3,128,256]{3,2,1,0:T(8,128)(2,1)S(1)}, u32[]{:S(2)}, u32[]{:S(2)}) async-start(bf16[8,3,128,256]{3,2,1,0:T(8,128)(2,1)} %pad_maximum_fusion), calls=%async_computation | async-start | bytes 3145728 | tf_op jit(solution)/shard_map/all_to_all | solution.py:185
  27.2 1.0 copy-start.6
  56.4 60.7 %all-to-all-start.1 = ((bf16[8,3,128,256]{3,2,1,0:T(8,128)(2,1)}), bf16[8,3,128,256]{3,2,1,0:T(8,128)(2,1)S(1)}, u32[]{:S(2)}, u32[]{:S(2)}) async-start(bf16[8,3,128,256]{3,2,1,0:T(8,128)(2,1)} %pad_maximum_fusion.1), calls=%async_computation.1 | async-start | bytes 3145728 | tf_op jit(solution)/shard_map/all_to_all | solution.py:185
  71.6 71.7 %all-gather.2.cloned.1.call-start = ((), (), s32[]{:S(2)}) async-start(), calls=%async_computation.5 | async-start | bytes 1769472 | tf_op jit(solution)/shard_map/all_gather | solution.py:217
  76.7 51.4 %collective-permute-start = (bf16[128,1024]{1,0:T(8,128)(2,1)S(1)}, bf16[128,1024]{1,0:T(8,128)(2,1)}, u32[]{:S(2)}, u32[]{:S(2)}) collective-permute-start(bf16[128,1024]{1,0:T(8,128)(2,1)S(1)} %attend.2.refs_0_), channel_id=1, source_target_pairs={{0,2},{2,4},{4,6},{6,0},{1,3},{3,5},{5,7},{7,1},{8,10},{10,12},{12... | collective-permute-start | bytes 786440 | tf_op jit(solution)/shard_map/ppermute | solution.py:163
  81.0 51.4 %collective-permute-start.2 = (bf16[128,1024]{1,0:T(8,128)(2,1)S(1)}, bf16[128,1024]{1,0:T(8,128)(2,1)}, u32[]{:S(2)}, u32[]{:S(2)}) collective-permute-start(bf16[128,1024]{1,0:T(8,128)(2,1)S(1)} %attend.2.refs_0_), channel_id=1, source_target_pairs={{0,6},{2,0},{4,2},{6,4},{1,7},{3,1},{5,3},{7,5},{8,14},{10,8},{12,... | collective-permute-start | bytes 786440 | tf_op jit(solution)/shard_map/ppermute | solution.py:163
  88.5 43.8 %collective-permute-start.1 = (bf16[128,1024]{1,0:T(8,128)(2,1)}, bf16[128,1024]{1,0:T(8,128)(2,1)}, u32[]{:S(2)}, u32[]{:S(2)}) collective-permute-start(bf16[128,1024]{1,0:T(8,128)(2,1)} %attend.3.refs_1_), channel_id=1, source_target_pairs={{0,2},{2,4},{4,6},{6,0},{1,3},{3,5},{5,7},{7,1},{8,10},{10,12},{12... | collective-permute-start | bytes 786440 | tf_op jit(solution)/shard_map/ppermute | solution.py:163
  92.5 39.9 %collective-permute-start.3 = (bf16[128,1024]{1,0:T(8,128)(2,1)}, bf16[128,1024]{1,0:T(8,128)(2,1)}, u32[]{:S(2)}, u32[]{:S(2)}) collective-permute-start(bf16[128,1024]{1,0:T(8,128)(2,1)} %attend.3.refs_1_), channel_id=1, source_target_pairs={{0,6},{2,0},{4,2},{6,4},{1,7},{3,1},{5,3},{7,5},{8,14},{10,8},{12,... | collective-permute-start | bytes 786440 | tf_op jit(solution)/shard_map/ppermute | solution.py:163
  132.4 23.8 %collective-permute-start.6 = (bf16[1024,256]{1,0:T(8,128)(2,1)}, bf16[1024,256]{1,0:T(8,128)(2,1)S(1)}, u32[]{:S(2)}, u32[]{:S(2)}) collective-permute-start(bf16[1024,256]{1,0:T(8,128)(2,1)} %tangent.1.refs_8_), channel_id=1, source_target_pairs={{0,1},{1,0},{2,3},{3,2},{4,5},{5,4},{6,7},{7,6},{8,9},{9,8},{10,11... | collective-permute-start | bytes 1572872 | tf_op jit(solution)/shard_map/ppermute | solution.py:167
  135.2 15.7 %collective-permute-start.4 = (bf16[128,1024]{1,0:T(8,128)(2,1)}, bf16[128,1024]{1,0:T(8,128)(2,1)S(1)}, u32[]{:S(2)}, u32[]{:S(2)}) collective-permute-start(bf16[128,1024]{1,0:T(8,128)(2,1)} %collective-permute-done.refs_2_), channel_id=1, source_target_pairs={{0,2},{2,4},{4,6},{6,0},{1,3},{3,5},{5,7},{7,1},{8,10},{10,12},{12... | collective-permute-start | bytes 786440 | tf_op jit(solution)/shard_map/ppermute | solution.py:163
  139.1 16.4 %collective-permute-start.5 = (bf16[128,1024]{1,0:T(8,128)(2,1)}, bf16[128,1024]{1,0:T(8,128)(2,1)S(1)}, u32[]{:S(2)}, u32[]{:S(2)}) collective-permute-start(bf16[128,1024]{1,0:T(8,128)(2,1)} %collective-permute-done.3.refs_5_), channel_id=1, source_target_pairs={{0,6},{2,0},{4,2},{6,4},{1,7},{3,1},{5,3},{7,5},{8,14},{10,8},{12,... | collective-permute-start | bytes 786440 | tf_op jit(solution)/shard_map/ppermute | solution.py:163
  155.5 0.7 copy-start.1
  156.2 1.0 copy-start.2
  180.3 37.9 %copy-start = (bf16[2048,384]{1,0:T(8,128)(2,1)S(1)}, bf16[2048,384]{1,0:T(8,128)(2,1)}, u32[]{:S(2)}) copy-start(bf16[2048,384]{1,0:T(8,128)(2,1)} %all-gather.2.cloned.1.call-done) | copy-start | bytes 4718596
  196.7 7.5 %collective-permute-start.7 = (f32[32,256]{1,0:T(8,128)S(1)}, f32[32,256]{1,0:T(8,128)S(1)}, u32[]{:S(2)}, u32[]{:S(2)}) collective-permute-start(f32[32,256]{1,0:T(8,128)S(1)} %reduce_sum.19), channel_id=1, source_target_pairs={{1,64},{64,1},{129,192},{192,129},{257,320},{320,257},{385,448},{4... | collective-permute-start | bytes 98312 | tf_op jit(solution)/shard_map/ppermute | solution.py:179
Sparse Core Ops, SparseCore 0:
  74.5 39.2 all-gather.1

commit v3 on v2

--- a/solution.py
+++ b/solution.py
@@ -210,9 +210,10 @@
 
     qkv = by_heads((queries, keys, values), seq_count)
     d_qkv = by_heads((d_queries, d_keys, d_values), seq_count)
-    pair = lax.all_gather(out_weight, "zl", axis=0, tiled=True)
-    qkv, pair = lax.optimization_barrier((qkv, pair))
-    weight_part = lax.all_gather(pair, "x", axis=0, tiled=True)
+    weight_part = lax.all_gather(out_weight, "x", axis=0)
+    d_qkv, weight_part = lax.optimization_barrier((d_qkv, weight_part))
+    weight_part = lax.all_gather(weight_part, "zl", axis=1)
+    weight_part = weight_part.reshape(-1, out_weight.shape[1])
     d_qkv, weight_part = lax.optimization_barrier((d_qkv, weight_part))
     weight_all = lax.all_gather(weight_part, "y", axis=0, tiled=True)
     qkv, d_qkv = exchange(qkv, SEQ), exchange(d_qkv, SEQ)

time: 228 us -> 223 us (0.978)
  blocking collectives: 64.2 us -> 86.8 us
  waiting for transfers between devices: 51.3 us -> 30.3 us
  starting transfers between devices: 57.7 us -> 50.8 us
    all_to_all x2, waiting for transfers between devices: 33.3 us -> 4.93 us  [exchange(): return lax.all_to_all(x, axes, split_axis=0, concat_axis=0, tiled=True)]
    all_gather x2, blocking collectives: 15.7 us -> 32.2 us  [the longest x1 21.9 us: shards(): weight_part = lax.all_gather(weight_part, 'zl', axis=1)]
    all_to_all x2, starting transfers between devices: 26.8 us -> 18.5 us  [exchange(): return lax.all_to_all(x, axes, split_axis=0, concat_axis=0, tiled=True)]
    ppermute x6, waiting for transfers between devices: 15.7 us -> 23 us  [shift(): return lax.ppermute(x, 'zh', [(i, (i + step) % n) for i in range(n)])]
    all_to_all x3, blocking collectives: 48.6 us -> 54.6 us  [exchange(): return lax.all_to_all(x, axes, split_axis=0, concat_axis=0, tiled=True)]
  transfers between devices with their start and end apart: 11 -> 11, of which waited for: 6 -> 5; matrix products, arithmetic and copies ran while one was open for 3% -> 3% of each run, Pallas kernels for 8% -> 9%
where the time goes in v3:
time: 223 us; the launch traced here: 221 us
  blocking collectives  86.8 us (39%)
  starting transfers between devices  50.8 us (23%)
  waiting for transfers between devices  30.3 us (14%)
  Pallas kernels  23.2 us (10%)
  between operations  15.6 us (7%)
  local copies, waits for them, and re-layouts  9.61 us (4%)
  other arithmetic  4.62 us (2%)
    all_to_all x3, blocking collectives, exchange(): return lax.all_to_all(x, axes, split_axis=0, concat_axis=0, tiled=True)  54.6 us
    ppermute x6, waiting for transfers between devices, shift(): return lax.ppermute(x, 'zh', [(i, (i + step) % n) for i in range(n)])  23 us
    ppermute x6, starting transfers between devices, shift(): return lax.ppermute(x, 'zh', [(i, (i + step) % n) for i in range(n)])  22.2 us
    all_gather x1, blocking collectives, shards(): weight_part = lax.all_gather(weight_part, 'zl', axis=1)  21.9 us
    all_to_all x2, starting transfers between devices, exchange(): return lax.all_to_all(x, axes, split_axis=0, concat_axis=0, tiled=True)  18.5 us
    pallas_call x1, Pallas kernels, attend_tangent(): pl.pallas_call(functools.partial(tangent_kernel, scale), grid=(width // H...  11 us
    all_gather x1, blocking collectives, shards(): weight_part = lax.all_gather(out_weight, 'x', axis=0)  10.3 us
    pallas_call x2, Pallas kernels, attend(): pl.pallas_call(functools.partial(forward_kernel, scale), grid=(1, length...  8.19 us
  transfers between devices with their start and end apart: 11, of which 5 were waited for; matrix products, arithmetic and copies ran while one was open for 3% of the time, Pallas kernels for 9%

profile of v3, /device:TPU:1, one launch (start us, length us, event | category | flops | bytes accessed | tf_op | source)
XLA Modules:
  0.0 220.9 jit_solution(9870901918969664930)
XLA Ops:
  6.5 1.4 copy.26
  7.9 0.2 copy.27
  8.2 0.3 copy.22
  8.4 0.2 copy.23
  8.7 0.3 copy-done.4
  9.0 0.3 copy.24
  9.2 0.2 copy.25
  9.5 1.3 pad_maximum_fusion
  10.8 11.9 %all-to-all-start = ((bf16[8,3,128,256]{3,2,1,0:T(8,128)(2,1)}), bf16[8,3,128,256]{3,2,1,0:T(8,128)(2,1)S(1)}, u32[]{:S(2)}, u32[]{:S(2)}) async-start(bf16[8,3,128,256]{3,2,1,0:T(8,128)(2,1)} %pad_maximum_fusion), calls=%async_computation | async-start | bytes 3145728 | tf_op jit(solution)/shard_map/all_to_all | solution.py:185
  22.7 0.3 copy.28
  23.0 0.2 copy.29
  23.2 0.5 copy-done.6
  23.8 0.3 copy.30
  24.1 0.2 copy.31
  24.3 1.3 copy.32
  25.6 1.0 copy.33
  26.6 10.3 %all-gather = bf16[128,384]{1,0:T(8,128)(2,1)S(1)} all-gather(bf16[32,384]{1,0:T(8,128)(2,1)S(1)} %copy-done.7), channel_id=2, replica_groups=mesh['y'=8,'x'=4,'zl'=2,'zh'=4,'core'=2] {'x'}, dimensions={0}, use_global_device_ids=true | all-gather | bytes 122880 | tf_op jit(solution)/shard_map/all_gather | solution.py:213
  36.9 2.3 %pad_maximum_fusion.1 = bf16[8,3,128,256]{3,2,1,0:T(8,128)(2,1)} fusion(bf16[8,1,128,256]{3,2,1,0:T(8,128)(2,1)} %bitcast.42, bf16[8,1,128,256]{3,2,1,0:T(8,128)(2,1)S(1)} %bitcast.40, bf16[8,1,128,256]{3,2,1,0:T(8,128)(2,1)S(1)} %bitcast.38), kind=kLoop, calls=%fused_computation.4 | loop fusion | flops 1572864 | bytes 3145728 | tf_op jit(solution)/shard_map/stack | solution.py:189
  39.2 21.9 %all-gather.1 = bf16[4,64,384]{2,1,0:T(8,128)(2,1)} all-gather(bf16[4,32,384]{2,1,0:T(8,128)(2,1)S(1)} %bitcast.46), channel_id=3, replica_groups=mesh['y'=8,'x'=4,'zl'=2,'zh'=4,'core'=2] {'zl'}, dimensions={1}, use_global_device_ids=true | all-gather | bytes 294912 | tf_op jit(solution)/shard_map/all_gather | solution.py:215
  61.2 6.6 %all-to-all-start.1 = ((bf16[8,3,128,256]{3,2,1,0:T(8,128)(2,1)}), bf16[8,3,128,256]{3,2,1,0:T(8,128)(2,1)S(1)}, u32[]{:S(2)}, u32[]{:S(2)}) async-start(bf16[8,3,128,256]{3,2,1,0:T(8,128)(2,1)} %pad_maximum_fusion.1), calls=%async_computation.1 | async-start | bytes 3145728 | tf_op jit(solution)/shard_map/all_to_all | solution.py:185
  67.7 0.7 all-gather.4.cloned.1.call-update
  69.1 3.8 %attend.2.refs_0_ = bf16[128,1024]{1,0:T(8,128)(2,1)S(1)} custom-call(bf16[8,3,128,256]{3,2,1,0:T(8,128)(2,1)S(1)} %all-to-all-done.q_ref.k_ref.v_ref, bf16[8,3,128,256]{3,2,1,0:T(8,128)(2,1)S(1)} %all-to-all-done.q_ref.k_ref.v_ref, bf16[8,3,128,256]{3,2,1,0:T(8,128)(2,1)S(1)} %all-to-all-done.q_ref.k_ref.v_ref), custom_call_target="tpu_custom_call" | custom-call | flops 536870912 | bytes 2097152 | tf_op jit(solution)/shard_map/attend/pallas_call | solution.py:75
  72.9 4.2 %collective-permute-start = (bf16[128,1024]{1,0:T(8,128)(2,1)S(1)}, bf16[128,1024]{1,0:T(8,128)(2,1)}, u32[]{:S(2)}, u32[]{:S(2)}) collective-permute-start(bf16[128,1024]{1,0:T(8,128)(2,1)S(1)} %attend.2.refs_0_), channel_id=1, source_target_pairs={{0,2},{2,4},{4,6},{6,0},{1,3},{3,5},{5,7},{7,1},{8,10},{10,12},{12... | collective-permute-start | bytes 786440 | tf_op jit(solution)/shard_map/ppermute | solution.py:163
  77.1 3.2 %collective-permute-start.2 = (bf16[128,1024]{1,0:T(8,128)(2,1)S(1)}, bf16[128,1024]{1,0:T(8,128)(2,1)}, u32[]{:S(2)}, u32[]{:S(2)}) collective-permute-start(bf16[128,1024]{1,0:T(8,128)(2,1)S(1)} %attend.2.refs_0_), channel_id=1, source_target_pairs={{0,6},{2,0},{4,2},{6,4},{1,7},{3,1},{5,3},{7,5},{8,14},{10,8},{12,... | collective-permute-start | bytes 786440 | tf_op jit(solution)/shard_map/ppermute | solution.py:163
  80.3 4.4 %attend.3.refs_1_ = bf16[128,1024]{1,0:T(8,128)(2,1)} custom-call(bf16[8,3,128,256]{3,2,1,0:T(8,128)(2,1)S(1)} %all-to-all-done.q_ref.k_ref.v_ref, bf16[8,3,128,256]{3,2,1,0:T(8,128)(2,1)S(1)} %all-to-all-done.q_ref.k_ref.v_ref, bf16[8,3,128,256]{3,2,1,0:T(8,128)(2,1)S(1)} %all-to-all-done.q_ref.k_ref.v_ref), custom_call_target="tpu_custom_call" | custom-call | flops 536870912 | bytes 2097152 | tf_op jit(solution)/shard_map/attend/pallas_call | solution.py:75
  84.7 3.9 %collective-permute-start.1 = (bf16[128,1024]{1,0:T(8,128)(2,1)}, bf16[128,1024]{1,0:T(8,128)(2,1)}, u32[]{:S(2)}, u32[]{:S(2)}) collective-permute-start(bf16[128,1024]{1,0:T(8,128)(2,1)} %attend.3.refs_1_), channel_id=1, source_target_pairs={{0,2},{2,4},{4,6},{6,0},{1,3},{3,5},{5,7},{7,1},{8,10},{10,12},{12... | collective-permute-start | bytes 786440 | tf_op jit(solution)/shard_map/ppermute | solution.py:163
  88.6 3.5 %collective-permute-start.3 = (bf16[128,1024]{1,0:T(8,128)(2,1)}, bf16[128,1024]{1,0:T(8,128)(2,1)}, u32[]{:S(2)}, u32[]{:S(2)}) collective-permute-start(bf16[128,1024]{1,0:T(8,128)(2,1)} %attend.3.refs_1_), channel_id=1, source_target_pairs={{0,6},{2,0},{4,2},{6,4},{1,7},{3,1},{5,3},{7,5},{8,14},{10,8},{12,... | collective-permute-start | bytes 786440 | tf_op jit(solution)/shard_map/ppermute | solution.py:163
  92.1 4.9 %all-to-all-done.1.dq_ref.dk_ref.dv_ref = bf16[8,3,128,256]{3,2,1,0:T(8,128)(2,1)S(1)} async-done(((bf16[8,3,128,256]{3,2,1,0:T(8,128)(2,1)}), bf16[8,3,128,256]{3,2,1,0:T(8,128)(2,1)S(1)}, u32[]{:S(2)}, u32[]{:S(2)}) %all-to-all-start.1) | async-done | bytes 1572896 | tf_op jit(solution)/shard_map/all_to_all | solution.py:185
  97.0 11.0 %tangent.1.refs_8_ = bf16[1024,256]{1,0:T(8,128)(2,1)} custom-call(f32[1]{0:T(128)S(6)} %copy.34.coef_ref, bf16[8,3,128,256]{3,2,1,0:T(8,128)(2,1)S(1)} %all-to-all-done.q_ref.k_ref.v_ref, bf16[8,3,128,256]{3,2,1,0:T(8,128)(2,1)S(1)} %all-to-all-done.q_ref.k_ref.v_ref, bf16[8,3,128,256]{3,2,1,0:T(8,128)(2,1)S(1)} %all-to-all-done.q_ref.k_ref.v_ref, ...), custom_call_target="tpu_custom_call" | custom-call | flops 3758096384 | bytes 8388608 | tf_op jit(solution)/shard_map/tangent/pallas_call | solution.py:92
  108.1 2.2 collective-permute-done.1.refs_3_
  110.3 11.9 %collective-permute-done.3.refs_5_ = bf16[128,1024]{1,0:T(8,128)(2,1)} collective-permute-done((bf16[128,1024]{1,0:T(8,128)(2,1)}, bf16[128,1024]{1,0:T(8,128)(2,1)}, u32[]{:S(2)}, u32[]{:S(2)}) %collective-permute-start.3) | collective-permute-done | bytes 262176 | tf_op jit(solution)/shard_map/ppermute | solution.py:163
  122.2 4.7 %collective-permute-start.6 = (bf16[1024,256]{1,0:T(8,128)(2,1)}, bf16[1024,256]{1,0:T(8,128)(2,1)S(1)}, u32[]{:S(2)}, u32[]{:S(2)}) collective-permute-start(bf16[1024,256]{1,0:T(8,128)(2,1)} %tangent.1.refs_8_), channel_id=1, source_target_pairs={{0,1},{1,0},{2,3},{3,2},{4,5},{5,4},{6,7},{7,6},{8,9},{9,8},{10,11... | collective-permute-start | bytes 1572872 | tf_op jit(solution)/shard_map/ppermute | solution.py:167
  126.9 4.3 %collective-permute-start.4 = (bf16[128,1024]{1,0:T(8,128)(2,1)}, bf16[128,1024]{1,0:T(8,128)(2,1)S(1)}, u32[]{:S(2)}, u32[]{:S(2)}) collective-permute-start(bf16[128,1024]{1,0:T(8,128)(2,1)} %collective-permute-done.refs_2_), channel_id=1, source_target_pairs={{0,2},{2,4},{4,6},{6,0},{1,3},{3,5},{5,7},{7,1},{8,10},{10,12},{12... | collective-permute-start | bytes 786440 | tf_op jit(solution)/shard_map/ppermute | solution.py:163
  131.2 3.1 %collective-permute-start.5 = (bf16[128,1024]{1,0:T(8,128)(2,1)}, bf16[128,1024]{1,0:T(8,128)(2,1)S(1)}, u32[]{:S(2)}, u32[]{:S(2)}) collective-permute-start(bf16[128,1024]{1,0:T(8,128)(2,1)} %collective-permute-done.3.refs_5_), channel_id=1, source_target_pairs={{0,6},{2,0},{4,2},{6,4},{1,7},{3,1},{5,3},{7,5},{8,14},{10,8},{12,... | collective-permute-start | bytes 786440 | tf_op jit(solution)/shard_map/ppermute | solution.py:163
  135.1 0.7 slice.16.refs_10_
  135.7 8.9 %collective-permute-done.4.refs_6_ = bf16[128,1024]{1,0:T(8,128)(2,1)S(1)} collective-permute-done((bf16[128,1024]{1,0:T(8,128)(2,1)}, bf16[128,1024]{1,0:T(8,128)(2,1)S(1)}, u32[]{:S(2)}, u32[]{:S(2)}) %collective-permute-start.4) | collective-permute-done | bytes 262176 | tf_op jit(solution)/shard_map/ppermute | solution.py:163
  144.7 0.7 copy-done.1
  145.4 0.9 copy-done.2
  146.3 2.8 %gram.1 = f32[8,264,256]{2,1,0:T(8,128)S(1)} custom-call(f32[1]{0:T(128)S(6)} %copy.35.weight_ref, s32[2]{0:T(128)S(1)} %pad_add_fusion.at_ref, bf16[128,1024]{1,0:T(8,128)(2,1)S(1)} %attend.2.refs_0_, bf16[128,1024]{1,0:T(8,128)(2,1)} %attend.3.refs_1_, bf16[128,1024]{1,0:T(8,128)(2,1)} %collective-permute-done.refs_2_, ...), custom_call_target="tpu_custom_call" | custom-call | tf_op jit(solution)/shard_map/gram/pallas_call | solution.py:133
  149.2 0.5 slice.17
  150.4 0.3 select_convert_fusion
  150.7 23.2 %all_to_all.25 = f16[8,264,256]{2,1,0:T(8,128)(2,1)S(1)} all-to-all(f16[8,264,256]{2,1,0:T(8,128)(2,1)S(1)} %select_convert_fusion), channel_id=1, replica_groups=mesh['y'=8,'x'=4,'zl'=2,'zh'=4,'core'=2] {'x','zl'}, dimensions={0} | all-to-all | bytes 2162688 | tf_op jit(solution)/shard_map/all_to_all | solution.py:185
  174.1 0.2 fusion
  174.4 16.2 %all_to_all.26 = f32[8,32,256]{2,1,0:T(8,128)S(1)} all-to-all(f32[8,32,256]{2,1,0:T(8,128)S(1)} %bitcast.44), channel_id=1, replica_groups=mesh['y'=8,'x'=4,'zl'=2,'zh'=4,'core'=2] {'y'}, dimensions={0} | all-to-all | bytes 524288 | tf_op jit(solution)/shard_map/all_to_all | solution.py:185
  190.6 5.4 %collective-permute-start.7 = (f32[32,256]{1,0:T(8,128)S(1)}, f32[32,256]{1,0:T(8,128)S(1)}, u32[]{:S(2)}, u32[]{:S(2)}) collective-permute-start(f32[32,256]{1,0:T(8,128)S(1)} %reduce_sum.19), channel_id=1, source_target_pairs={{1,64},{64,1},{129,192},{192,129},{257,320},{320,257},{385,448},{4... | collective-permute-start | bytes 98312 | tf_op jit(solution)/shard_map/ppermute | solution.py:179
  196.1 1.6 collective-permute-done.7
  197.7 15.2 %all_to_all.27.g_ref = f32[8,32,256]{2,1,0:T(8,128)S(1)} all-to-all(f32[8,32,256]{2,1,0:T(8,128)S(1)} %broadcast_in_dim.11), channel_id=1, replica_groups=mesh['y'=8,'x'=4,'zl'=2,'zh'=4,'core'=2] {'zh','core'}, dimensions={0} | all-to-all | bytes 524288 | tf_op jit(solution)/shard_map/all_to_all | solution.py:185
  212.9 1.2 finish.1
  (26 shorter events, 0.5 us)
Async XLA Ops:
  6.5 1.6 copy-start.3
  7.9 1.0 copy-start.4
  10.8 11.9 %copy-start.5 = (bf16[128,2048]{1,0:T(8,128)(2,1)S(1)}, bf16[128,2048]{1,0:T(8,128)(2,1)}, u32[]{:S(2)}) copy-start(bf16[128,2048]{1,0:T(8,128)(2,1)} %param.12) | copy-start | bytes 1572868
  10.8 50.4 %all-to-all-start = ((bf16[8,3,128,256]{3,2,1,0:T(8,128)(2,1)}), bf16[8,3,128,256]{3,2,1,0:T(8,128)(2,1)S(1)}, u32[]{:S(2)}, u32[]{:S(2)}) async-start(bf16[8,3,128,256]{3,2,1,0:T(8,128)(2,1)} %pad_maximum_fusion), calls=%async_computation | async-start | bytes 3145728 | tf_op jit(solution)/shard_map/all_to_all | solution.py:185
  22.7 1.0 copy-start.6
  24.1 2.6 %copy-start.7 = (bf16[32,384]{1,0:T(8,128)(2,1)S(1)}, bf16[32,384]{1,0:T(8,128)(2,1)}, u32[]{:S(2)}) copy-start(bf16[32,384]{1,0:T(8,128)(2,1)} %param.15) | copy-start | bytes 73732
  61.2 35.9 %all-to-all-start.1 = ((bf16[8,3,128,256]{3,2,1,0:T(8,128)(2,1)}), bf16[8,3,128,256]{3,2,1,0:T(8,128)(2,1)S(1)}, u32[]{:S(2)}, u32[]{:S(2)}) async-start(bf16[8,3,128,256]{3,2,1,0:T(8,128)(2,1)} %pad_maximum_fusion.1), calls=%async_computation.1 | async-start | bytes 3145728 | tf_op jit(solution)/shard_map/all_to_all | solution.py:185
  67.7 67.3 %all-gather.4.cloned.1.call-start = ((), (), s32[]{:S(2)}) async-start(), calls=%async_computation.5 | async-start | bytes 1769472 | tf_op jit(solution)/shard_map/all_gather | solution.py:218
  72.9 35.1 %collective-permute-start = (bf16[128,1024]{1,0:T(8,128)(2,1)S(1)}, bf16[128,1024]{1,0:T(8,128)(2,1)}, u32[]{:S(2)}, u32[]{:S(2)}) collective-permute-start(bf16[128,1024]{1,0:T(8,128)(2,1)S(1)} %attend.2.refs_0_), channel_id=1, source_target_pairs={{0,2},{2,4},{4,6},{6,0},{1,3},{3,5},{5,7},{7,1},{8,10},{10,12},{12... | collective-permute-start | bytes 786440 | tf_op jit(solution)/shard_map/ppermute | solution.py:163
  77.1 33.1 %collective-permute-start.2 = (bf16[128,1024]{1,0:T(8,128)(2,1)S(1)}, bf16[128,1024]{1,0:T(8,128)(2,1)}, u32[]{:S(2)}, u32[]{:S(2)}) collective-permute-start(bf16[128,1024]{1,0:T(8,128)(2,1)S(1)} %attend.2.refs_0_), channel_id=1, source_target_pairs={{0,6},{2,0},{4,2},{6,4},{1,7},{3,1},{5,3},{7,5},{8,14},{10,8},{12,... | collective-permute-start | bytes 786440 | tf_op jit(solution)/shard_map/ppermute | solution.py:163
  84.7 25.5 %collective-permute-start.1 = (bf16[128,1024]{1,0:T(8,128)(2,1)}, bf16[128,1024]{1,0:T(8,128)(2,1)}, u32[]{:S(2)}, u32[]{:S(2)}) collective-permute-start(bf16[128,1024]{1,0:T(8,128)(2,1)} %attend.3.refs_1_), channel_id=1, source_target_pairs={{0,2},{2,4},{4,6},{6,0},{1,3},{3,5},{5,7},{7,1},{8,10},{10,12},{12... | collective-permute-start | bytes 786440 | tf_op jit(solution)/shard_map/ppermute | solution.py:163
  88.6 33.5 %collective-permute-start.3 = (bf16[128,1024]{1,0:T(8,128)(2,1)}, bf16[128,1024]{1,0:T(8,128)(2,1)}, u32[]{:S(2)}, u32[]{:S(2)}) collective-permute-start(bf16[128,1024]{1,0:T(8,128)(2,1)} %attend.3.refs_1_), channel_id=1, source_target_pairs={{0,6},{2,0},{4,2},{6,4},{1,7},{3,1},{5,3},{7,5},{8,14},{10,8},{12,... | collective-permute-start | bytes 786440 | tf_op jit(solution)/shard_map/ppermute | solution.py:163
  122.2 23.2 %collective-permute-start.6 = (bf16[1024,256]{1,0:T(8,128)(2,1)}, bf16[1024,256]{1,0:T(8,128)(2,1)S(1)}, u32[]{:S(2)}, u32[]{:S(2)}) collective-permute-start(bf16[1024,256]{1,0:T(8,128)(2,1)} %tangent.1.refs_8_), channel_id=1, source_target_pairs={{0,1},{1,0},{2,3},{3,2},{4,5},{5,4},{6,7},{7,6},{8,9},{9,8},{10,11... | collective-permute-start | bytes 1572872 | tf_op jit(solution)/shard_map/ppermute | solution.py:167
  126.9 17.8 %collective-permute-start.4 = (bf16[128,1024]{1,0:T(8,128)(2,1)}, bf16[128,1024]{1,0:T(8,128)(2,1)S(1)}, u32[]{:S(2)}, u32[]{:S(2)}) collective-permute-start(bf16[128,1024]{1,0:T(8,128)(2,1)} %collective-permute-done.refs_2_), channel_id=1, source_target_pairs={{0,2},{2,4},{4,6},{6,0},{1,3},{3,5},{5,7},{7,1},{8,10},{10,12},{12... | collective-permute-start | bytes 786440 | tf_op jit(solution)/shard_map/ppermute | solution.py:163
  131.2 13.5 %collective-permute-start.5 = (bf16[128,1024]{1,0:T(8,128)(2,1)}, bf16[128,1024]{1,0:T(8,128)(2,1)S(1)}, u32[]{:S(2)}, u32[]{:S(2)}) collective-permute-start(bf16[128,1024]{1,0:T(8,128)(2,1)} %collective-permute-done.3.refs_5_), channel_id=1, source_target_pairs={{0,6},{2,0},{4,2},{6,4},{1,7},{3,1},{5,3},{7,5},{8,14},{10,8},{12,... | collective-permute-start | bytes 786440 | tf_op jit(solution)/shard_map/ppermute | solution.py:163
  144.7 0.7 copy-start.1
  145.4 1.0 copy-start.2
  174.1 38.7 %copy-start = (bf16[2048,384]{1,0:T(8,128)(2,1)S(1)}, bf16[2048,384]{1,0:T(8,128)(2,1)}, u32[]{:S(2)}) copy-start(bf16[2048,384]{1,0:T(8,128)(2,1)} %all-gather.4.cloned.1.call-done) | copy-start | bytes 4718596
  190.6 7.0 %collective-permute-start.7 = (f32[32,256]{1,0:T(8,128)S(1)}, f32[32,256]{1,0:T(8,128)S(1)}, u32[]{:S(2)}, u32[]{:S(2)}) collective-permute-start(f32[32,256]{1,0:T(8,128)S(1)} %reduce_sum.19), channel_id=1, source_target_pairs={{1,64},{64,1},{129,192},{192,129},{257,320},{320,257},{385,448},{4... | collective-permute-start | bytes 98312 | tf_op jit(solution)/shard_map/ppermute | solution.py:179
Sparse Core Ops, SparseCore 0:
  70.6 39.3 all-gather.3

commit v4 on v3

--- a/solution.py
+++ b/solution.py
@@ -181,6 +181,14 @@
     return jnp.where(stays, x, moved)
 
 
+def gather_rows(x):
+    mine = exchange(jnp.broadcast_to(x[None], (lax.axis_size("zh"),) + x.shape), "zh")
+    theirs = swap(mine)
+    first = lax.axis_index("core") == 0
+    pair = (jnp.where(first, mine, theirs), jnp.where(first, theirs, mine))
+    return jnp.stack(pair, axis=1).reshape((-1,) + x.shape)
+
+
 def exchange(x, axes):
     return lax.all_to_all(x, axes, split_axis=0, concat_axis=0, tiled=True)
 
@@ -233,7 +241,7 @@
     term = gram(loss_weight, blocks, mixed_pair, lax.axis_size(NEAR), weight_all[:16, :HEAD])
     summed = reduce_near(term).reshape(lax.axis_size("y"), -1, mixed.shape[1])
     summed = settle(jnp.sum(exchange(summed, "y"), axis=0))
-    rows = exchange(jnp.broadcast_to(summed[None], (seq_count,) + summed.shape), SEQ)
+    rows = gather_rows(summed)
     total_tokens = length * dp_count
     return finish(
         rows, weight_all.reshape(seq_count, mixed.shape[1], -1), LOSS_SCALE / total_tokens**0.5

time: 223 us -> 223 us (level)
  blocking collectives: 86.8 us -> 83.4 us
    all_to_all x3, blocking collectives: 54.6 us -> 51.2 us  [exchange(): return lax.all_to_all(x, axes, split_axis=0, concat_axis=0, tiled=True)]
    ppermute x1 -> x2, starting transfers between devices: 4.72 us -> 6.63 us  [swap(): return lax.ppermute(x, 'core', [(0, 1), (1, 0)])]
  transfers between devices with their start and end apart: 11 -> 12, of which waited for: 5 -> 6; matrix products, arithmetic and copies ran while one was open for 3% -> 3% of each run, Pallas kernels for 9% -> 9%
where the time goes in v4:
time: 223 us; the launch traced here: 221 us
  blocking collectives  83.4 us (37%)
  starting transfers between devices  52.7 us (24%)
  waiting for transfers between devices  31.6 us (14%)
  Pallas kernels  23.2 us (10%)
  between operations  15.7 us (7%)
  local copies, waits for them, and re-layouts  9.67 us (4%)
  other arithmetic  4.68 us (2%)
    all_to_all x3, blocking collectives, exchange(): return lax.all_to_all(x, axes, split_axis=0, concat_axis=0, tiled=True)  51.2 us
    ppermute x6, waiting for transfers between devices, shift(): return lax.ppermute(x, 'zh', [(i, (i + step) % n) for i in range(n)])  23 us
    ppermute x6, starting transfers between devices, shift(): return lax.ppermute(x, 'zh', [(i, (i + step) % n) for i in range(n)])  22.2 us
    all_gather x1, blocking collectives, shards(): weight_part = lax.all_gather(weight_part, 'zl', axis=1)  21.9 us
    all_to_all x2, starting transfers between devices, exchange(): return lax.all_to_all(x, axes, split_axis=0, concat_axis=0, tiled=True)  18.5 us
    pallas_call x1, Pallas kernels, attend_tangent(): pl.pallas_call(functools.partial(tangent_kernel, scale), grid=(width // H...  11 us
    all_gather x1, blocking collectives, shards(): weight_part = lax.all_gather(out_weight, 'x', axis=0)  10.3 us
    pallas_call x2, Pallas kernels, attend(): pl.pallas_call(functools.partial(forward_kernel, scale), grid=(1, length...  8.18 us
  transfers between devices with their start and end apart: 12, of which 6 were waited for; matrix products, arithmetic and copies ran while one was open for 3% of the time, Pallas kernels for 9%

profile of v4, /device:TPU:1, one launch (start us, length us, event | category | flops | bytes accessed | tf_op | source)
XLA Modules:
  0.0 221.0 jit_solution(11385212967100573820)
XLA Ops:
  6.5 1.4 copy.28
  8.2 0.3 copy.24
  8.4 0.2 copy.25
  8.7 0.3 copy-done.4
  9.0 0.3 copy.26
  9.2 0.2 copy.27
  9.5 1.3 pad_maximum_fusion
  10.8 11.9 %all-to-all-start = ((bf16[8,3,128,256]{3,2,1,0:T(8,128)(2,1)}), bf16[8,3,128,256]{3,2,1,0:T(8,128)(2,1)S(1)}, u32[]{:S(2)}, u32[]{:S(2)}) async-start(bf16[8,3,128,256]{3,2,1,0:T(8,128)(2,1)} %pad_maximum_fusion), calls=%async_computation | async-start | bytes 3145728 | tf_op jit(solution)/shard_map/all_to_all | solution.py:193
  22.7 0.3 copy.30
  23.0 0.2 copy.31
  23.2 0.5 copy-done.6
  23.8 0.3 copy.32
  24.3 1.3 copy.34
  25.6 1.0 copy.35
  26.6 10.3 %all-gather = bf16[128,384]{1,0:T(8,128)(2,1)S(1)} all-gather(bf16[32,384]{1,0:T(8,128)(2,1)S(1)} %copy-done.7), channel_id=2, replica_groups=mesh['y'=8,'x'=4,'zl'=2,'zh'=4,'core'=2] {'x'}, dimensions={0}, use_global_device_ids=true | all-gather | bytes 122880 | tf_op jit(solution)/shard_map/all_gather | solution.py:221
  36.9 2.4 %pad_maximum_fusion.1 = bf16[8,3,128,256]{3,2,1,0:T(8,128)(2,1)} fusion(bf16[8,1,128,256]{3,2,1,0:T(8,128)(2,1)} %bitcast.50, bf16[8,1,128,256]{3,2,1,0:T(8,128)(2,1)S(1)} %bitcast.48, bf16[8,1,128,256]{3,2,1,0:T(8,128)(2,1)S(1)} %bitcast.46), kind=kLoop, calls=%fused_computation.4 | loop fusion | flops 1572864 | bytes 3145728 | tf_op jit(solution)/shard_map/stack | solution.py:197
  39.2 21.9 %all-gather.1 = bf16[4,64,384]{2,1,0:T(8,128)(2,1)} all-gather(bf16[4,32,384]{2,1,0:T(8,128)(2,1)S(1)} %bitcast.54), channel_id=3, replica_groups=mesh['y'=8,'x'=4,'zl'=2,'zh'=4,'core'=2] {'zl'}, dimensions={1}, use_global_device_ids=true | all-gather | bytes 294912 | tf_op jit(solution)/shard_map/all_gather | solution.py:223
  61.2 6.6 %all-to-all-start.1 = ((bf16[8,3,128,256]{3,2,1,0:T(8,128)(2,1)}), bf16[8,3,128,256]{3,2,1,0:T(8,128)(2,1)S(1)}, u32[]{:S(2)}, u32[]{:S(2)}) async-start(bf16[8,3,128,256]{3,2,1,0:T(8,128)(2,1)} %pad_maximum_fusion.1), calls=%async_computation.1 | async-start | bytes 3145728 | tf_op jit(solution)/shard_map/all_to_all | solution.py:193
  67.7 0.7 all-gather.4.cloned.1.call-update
  69.1 3.8 %attend.2.refs_0_ = bf16[128,1024]{1,0:T(8,128)(2,1)S(1)} custom-call(bf16[8,3,128,256]{3,2,1,0:T(8,128)(2,1)S(1)} %all-to-all-done.q_ref.k_ref.v_ref, bf16[8,3,128,256]{3,2,1,0:T(8,128)(2,1)S(1)} %all-to-all-done.q_ref.k_ref.v_ref, bf16[8,3,128,256]{3,2,1,0:T(8,128)(2,1)S(1)} %all-to-all-done.q_ref.k_ref.v_ref), custom_call_target="tpu_custom_call" | custom-call | flops 536870912 | bytes 2097152 | tf_op jit(solution)/shard_map/attend/pallas_call | solution.py:75
  72.9 4.2 %collective-permute-start = (bf16[128,1024]{1,0:T(8,128)(2,1)S(1)}, bf16[128,1024]{1,0:T(8,128)(2,1)}, u32[]{:S(2)}, u32[]{:S(2)}) collective-permute-start(bf16[128,1024]{1,0:T(8,128)(2,1)S(1)} %attend.2.refs_0_), channel_id=1, source_target_pairs={{0,2},{2,4},{4,6},{6,0},{1,3},{3,5},{5,7},{7,1},{8,10},{10,12},{12... | collective-permute-start | bytes 786440 | tf_op jit(solution)/shard_map/ppermute | solution.py:163
  77.1 3.2 %collective-permute-start.2 = (bf16[128,1024]{1,0:T(8,128)(2,1)S(1)}, bf16[128,1024]{1,0:T(8,128)(2,1)}, u32[]{:S(2)}, u32[]{:S(2)}) collective-permute-start(bf16[128,1024]{1,0:T(8,128)(2,1)S(1)} %attend.2.refs_0_), channel_id=1, source_target_pairs={{0,6},{2,0},{4,2},{6,4},{1,7},{3,1},{5,3},{7,5},{8,14},{10,8},{12,... | collective-permute-start | bytes 786440 | tf_op jit(solution)/shard_map/ppermute | solution.py:163
  80.3 4.4 %attend.3.refs_1_ = bf16[128,1024]{1,0:T(8,128)(2,1)} custom-call(bf16[8,3,128,256]{3,2,1,0:T(8,128)(2,1)S(1)} %all-to-all-done.q_ref.k_ref.v_ref, bf16[8,3,128,256]{3,2,1,0:T(8,128)(2,1)S(1)} %all-to-all-done.q_ref.k_ref.v_ref, bf16[8,3,128,256]{3,2,1,0:T(8,128)(2,1)S(1)} %all-to-all-done.q_ref.k_ref.v_ref), custom_call_target="tpu_custom_call" | custom-call | flops 536870912 | bytes 2097152 | tf_op jit(solution)/shard_map/attend/pallas_call | solution.py:75
  84.7 3.9 %collective-permute-start.1 = (bf16[128,1024]{1,0:T(8,128)(2,1)}, bf16[128,1024]{1,0:T(8,128)(2,1)}, u32[]{:S(2)}, u32[]{:S(2)}) collective-permute-start(bf16[128,1024]{1,0:T(8,128)(2,1)} %attend.3.refs_1_), channel_id=1, source_target_pairs={{0,2},{2,4},{4,6},{6,0},{1,3},{3,5},{5,7},{7,1},{8,10},{10,12},{12... | collective-permute-start | bytes 786440 | tf_op jit(solution)/shard_map/ppermute | solution.py:163
  88.6 3.5 %collective-permute-start.3 = (bf16[128,1024]{1,0:T(8,128)(2,1)}, bf16[128,1024]{1,0:T(8,128)(2,1)}, u32[]{:S(2)}, u32[]{:S(2)}) collective-permute-start(bf16[128,1024]{1,0:T(8,128)(2,1)} %attend.3.refs_1_), channel_id=1, source_target_pairs={{0,6},{2,0},{4,2},{6,4},{1,7},{3,1},{5,3},{7,5},{8,14},{10,8},{12,... | collective-permute-start | bytes 786440 | tf_op jit(solution)/shard_map/ppermute | solution.py:163
  92.1 4.9 %all-to-all-done.1.dq_ref.dk_ref.dv_ref = bf16[8,3,128,256]{3,2,1,0:T(8,128)(2,1)S(1)} async-done(((bf16[8,3,128,256]{3,2,1,0:T(8,128)(2,1)}), bf16[8,3,128,256]{3,2,1,0:T(8,128)(2,1)S(1)}, u32[]{:S(2)}, u32[]{:S(2)}) %all-to-all-start.1) | async-done | bytes 1572896 | tf_op jit(solution)/shard_map/all_to_all | solution.py:193
  97.0 11.0 %tangent.1.refs_8_ = bf16[1024,256]{1,0:T(8,128)(2,1)} custom-call(f32[1]{0:T(128)S(6)} %copy.37.coef_ref, bf16[8,3,128,256]{3,2,1,0:T(8,128)(2,1)S(1)} %all-to-all-done.q_ref.k_ref.v_ref, bf16[8,3,128,256]{3,2,1,0:T(8,128)(2,1)S(1)} %all-to-all-done.q_ref.k_ref.v_ref, bf16[8,3,128,256]{3,2,1,0:T(8,128)(2,1)S(1)} %all-to-all-done.q_ref.k_ref.v_ref, ...), custom_call_target="tpu_custom_call" | custom-call | flops 3758096384 | bytes 8388608 | tf_op jit(solution)/shard_map/tangent/pallas_call | solution.py:92
  108.1 2.2 collective-permute-done.1.refs_3_
  110.3 11.9 %collective-permute-done.3.refs_5_ = bf16[128,1024]{1,0:T(8,128)(2,1)} collective-permute-done((bf16[128,1024]{1,0:T(8,128)(2,1)}, bf16[128,1024]{1,0:T(8,128)(2,1)}, u32[]{:S(2)}, u32[]{:S(2)}) %collective-permute-start.3) | collective-permute-done | bytes 262176 | tf_op jit(solution)/shard_map/ppermute | solution.py:163
  122.2 4.7 %collective-permute-start.6 = (bf16[1024,256]{1,0:T(8,128)(2,1)}, bf16[1024,256]{1,0:T(8,128)(2,1)S(1)}, u32[]{:S(2)}, u32[]{:S(2)}) collective-permute-start(bf16[1024,256]{1,0:T(8,128)(2,1)} %tangent.1.refs_8_), channel_id=1, source_target_pairs={{0,1},{1,0},{2,3},{3,2},{4,5},{5,4},{6,7},{7,6},{8,9},{9,8},{10,11... | collective-permute-start | bytes 1572872 | tf_op jit(solution)/shard_map/ppermute | solution.py:167
  126.9 4.3 %collective-permute-start.4 = (bf16[128,1024]{1,0:T(8,128)(2,1)}, bf16[128,1024]{1,0:T(8,128)(2,1)S(1)}, u32[]{:S(2)}, u32[]{:S(2)}) collective-permute-start(bf16[128,1024]{1,0:T(8,128)(2,1)} %collective-permute-done.refs_2_), channel_id=1, source_target_pairs={{0,2},{2,4},{4,6},{6,0},{1,3},{3,5},{5,7},{7,1},{8,10},{10,12},{12... | collective-permute-start | bytes 786440 | tf_op jit(solution)/shard_map/ppermute | solution.py:163
  131.2 3.1 %collective-permute-start.5 = (bf16[128,1024]{1,0:T(8,128)(2,1)}, bf16[128,1024]{1,0:T(8,128)(2,1)S(1)}, u32[]{:S(2)}, u32[]{:S(2)}) collective-permute-start(bf16[128,1024]{1,0:T(8,128)(2,1)} %collective-permute-done.3.refs_5_), channel_id=1, source_target_pairs={{0,6},{2,0},{4,2},{6,4},{1,7},{3,1},{5,3},{7,5},{8,14},{10,8},{12,... | collective-permute-start | bytes 786440 | tf_op jit(solution)/shard_map/ppermute | solution.py:163
  135.1 0.7 slice.16.refs_10_
  135.8 8.9 %collective-permute-done.4.refs_6_ = bf16[128,1024]{1,0:T(8,128)(2,1)S(1)} collective-permute-done((bf16[128,1024]{1,0:T(8,128)(2,1)}, bf16[128,1024]{1,0:T(8,128)(2,1)S(1)}, u32[]{:S(2)}, u32[]{:S(2)}) %collective-permute-start.4) | collective-permute-done | bytes 262176 | tf_op jit(solution)/shard_map/ppermute | solution.py:163
  144.7 0.7 copy-done.1
  145.4 0.9 copy-done.2
  146.3 2.8 %gram.1 = f32[8,264,256]{2,1,0:T(8,128)S(1)} custom-call(f32[1]{0:T(128)S(6)} %copy.38.weight_ref, s32[2]{0:T(128)S(1)} %pad_add_fusion.at_ref, bf16[128,1024]{1,0:T(8,128)(2,1)S(1)} %attend.2.refs_0_, bf16[128,1024]{1,0:T(8,128)(2,1)} %attend.3.refs_1_, bf16[128,1024]{1,0:T(8,128)(2,1)} %collective-permute-done.refs_2_, ...), custom_call_target="tpu_custom_call" | custom-call | tf_op jit(solution)/shard_map/gram/pallas_call | solution.py:133
  149.2 0.6 slice.17
  150.6 0.3 select_convert_fusion
  150.9 23.2 %all_to_all.25 = f16[8,264,256]{2,1,0:T(8,128)(2,1)S(1)} all-to-all(f16[8,264,256]{2,1,0:T(8,128)(2,1)S(1)} %select_convert_fusion), channel_id=1, replica_groups=mesh['y'=8,'x'=4,'zl'=2,'zh'=4,'core'=2] {'x','zl'}, dimensions={0} | all-to-all | bytes 2162688 | tf_op jit(solution)/shard_map/all_to_all | solution.py:193
  174.4 0.2 fusion
  174.6 16.2 %all_to_all.26 = f32[8,32,256]{2,1,0:T(8,128)S(1)} all-to-all(f32[8,32,256]{2,1,0:T(8,128)S(1)} %bitcast.52), channel_id=1, replica_groups=mesh['y'=8,'x'=4,'zl'=2,'zh'=4,'core'=2] {'y'}, dimensions={0} | all-to-all | bytes 524288 | tf_op jit(solution)/shard_map/all_to_all | solution.py:193
  190.8 5.4 %collective-permute-start.7 = (f32[32,256]{1,0:T(8,128)S(1)}, f32[32,256]{1,0:T(8,128)S(1)}, u32[]{:S(2)}, u32[]{:S(2)}) collective-permute-start(f32[32,256]{1,0:T(8,128)S(1)} %reduce_sum.19), channel_id=1, source_target_pairs={{1,64},{64,1},{129,192},{192,129},{257,320},{320,257},{385,448},{4... | collective-permute-start | bytes 98312 | tf_op jit(solution)/shard_map/ppermute | solution.py:179
  196.3 1.6 collective-permute-done.7
  197.9 11.8 %all_to_all.27 = f32[4,32,256]{2,1,0:T(8,128)S(1)} all-to-all(f32[4,32,256]{2,1,0:T(8,128)S(1)} %broadcast_in_dim.11), channel_id=1, replica_groups=mesh['y'=8,'x'=4,'zl'=2,'zh'=4,'core'=2] {'zh'}, dimensions={0} | all-to-all | bytes 262144 | tf_op jit(solution)/shard_map/all_to_all | solution.py:193
  209.7 1.9 collective-permute-start.8
  211.6 1.3 collective-permute-done.8
  213.0 1.2 finish.1
  (30 shorter events, 0.9 us)
Async XLA Ops:
  6.5 1.6 copy-start.3
  7.9 1.0 copy-start.4
  10.8 11.9 %copy-start.5 = (bf16[128,2048]{1,0:T(8,128)(2,1)S(1)}, bf16[128,2048]{1,0:T(8,128)(2,1)}, u32[]{:S(2)}) copy-start(bf16[128,2048]{1,0:T(8,128)(2,1)} %param.12) | copy-start | bytes 1572868
  10.8 50.4 %all-to-all-start = ((bf16[8,3,128,256]{3,2,1,0:T(8,128)(2,1)}), bf16[8,3,128,256]{3,2,1,0:T(8,128)(2,1)S(1)}, u32[]{:S(2)}, u32[]{:S(2)}) async-start(bf16[8,3,128,256]{3,2,1,0:T(8,128)(2,1)} %pad_maximum_fusion), calls=%async_computation | async-start | bytes 3145728 | tf_op jit(solution)/shard_map/all_to_all | solution.py:193
  22.7 1.0 copy-start.6
  24.1 2.6 %copy-start.7 = (bf16[32,384]{1,0:T(8,128)(2,1)S(1)}, bf16[32,384]{1,0:T(8,128)(2,1)}, u32[]{:S(2)}) copy-start(bf16[32,384]{1,0:T(8,128)(2,1)} %param.15) | copy-start | bytes 73732
  61.2 35.9 %all-to-all-start.1 = ((bf16[8,3,128,256]{3,2,1,0:T(8,128)(2,1)}), bf16[8,3,128,256]{3,2,1,0:T(8,128)(2,1)S(1)}, u32[]{:S(2)}, u32[]{:S(2)}) async-start(bf16[8,3,128,256]{3,2,1,0:T(8,128)(2,1)} %pad_maximum_fusion.1), calls=%async_computation.1 | async-start | bytes 3145728 | tf_op jit(solution)/shard_map/all_to_all | solution.py:193
  67.7 67.3 %all-gather.4.cloned.1.call-start = ((), (), s32[]{:S(2)}) async-start(), calls=%async_computation.5 | async-start | bytes 1769472 | tf_op jit(solution)/shard_map/all_gather | solution.py:226
  72.9 35.2 %collective-permute-start = (bf16[128,1024]{1,0:T(8,128)(2,1)S(1)}, bf16[128,1024]{1,0:T(8,128)(2,1)}, u32[]{:S(2)}, u32[]{:S(2)}) collective-permute-start(bf16[128,1024]{1,0:T(8,128)(2,1)S(1)} %attend.2.refs_0_), channel_id=1, source_target_pairs={{0,2},{2,4},{4,6},{6,0},{1,3},{3,5},{5,7},{7,1},{8,10},{10,12},{12... | collective-permute-start | bytes 786440 | tf_op jit(solution)/shard_map/ppermute | solution.py:163
  77.1 33.1 %collective-permute-start.2 = (bf16[128,1024]{1,0:T(8,128)(2,1)S(1)}, bf16[128,1024]{1,0:T(8,128)(2,1)}, u32[]{:S(2)}, u32[]{:S(2)}) collective-permute-start(bf16[128,1024]{1,0:T(8,128)(2,1)S(1)} %attend.2.refs_0_), channel_id=1, source_target_pairs={{0,6},{2,0},{4,2},{6,4},{1,7},{3,1},{5,3},{7,5},{8,14},{10,8},{12,... | collective-permute-start | bytes 786440 | tf_op jit(solution)/shard_map/ppermute | solution.py:163
  84.7 25.5 %collective-permute-start.1 = (bf16[128,1024]{1,0:T(8,128)(2,1)}, bf16[128,1024]{1,0:T(8,128)(2,1)}, u32[]{:S(2)}, u32[]{:S(2)}) collective-permute-start(bf16[128,1024]{1,0:T(8,128)(2,1)} %attend.3.refs_1_), channel_id=1, source_target_pairs={{0,2},{2,4},{4,6},{6,0},{1,3},{3,5},{5,7},{7,1},{8,10},{10,12},{12... | collective-permute-start | bytes 786440 | tf_op jit(solution)/shard_map/ppermute | solution.py:163
  88.6 33.6 %collective-permute-start.3 = (bf16[128,1024]{1,0:T(8,128)(2,1)}, bf16[128,1024]{1,0:T(8,128)(2,1)}, u32[]{:S(2)}, u32[]{:S(2)}) collective-permute-start(bf16[128,1024]{1,0:T(8,128)(2,1)} %attend.3.refs_1_), channel_id=1, source_target_pairs={{0,6},{2,0},{4,2},{6,4},{1,7},{3,1},{5,3},{7,5},{8,14},{10,8},{12,... | collective-permute-start | bytes 786440 | tf_op jit(solution)/shard_map/ppermute | solution.py:163
  122.2 23.2 %collective-permute-start.6 = (bf16[1024,256]{1,0:T(8,128)(2,1)}, bf16[1024,256]{1,0:T(8,128)(2,1)S(1)}, u32[]{:S(2)}, u32[]{:S(2)}) collective-permute-start(bf16[1024,256]{1,0:T(8,128)(2,1)} %tangent.1.refs_8_), channel_id=1, source_target_pairs={{0,1},{1,0},{2,3},{3,2},{4,5},{5,4},{6,7},{7,6},{8,9},{9,8},{10,11... | collective-permute-start | bytes 1572872 | tf_op jit(solution)/shard_map/ppermute | solution.py:167
  126.9 17.8 %collective-permute-start.4 = (bf16[128,1024]{1,0:T(8,128)(2,1)}, bf16[128,1024]{1,0:T(8,128)(2,1)S(1)}, u32[]{:S(2)}, u32[]{:S(2)}) collective-permute-start(bf16[128,1024]{1,0:T(8,128)(2,1)} %collective-permute-done.refs_2_), channel_id=1, source_target_pairs={{0,2},{2,4},{4,6},{6,0},{1,3},{3,5},{5,7},{7,1},{8,10},{10,12},{12... | collective-permute-start | bytes 786440 | tf_op jit(solution)/shard_map/ppermute | solution.py:163
  131.2 13.5 %collective-permute-start.5 = (bf16[128,1024]{1,0:T(8,128)(2,1)}, bf16[128,1024]{1,0:T(8,128)(2,1)S(1)}, u32[]{:S(2)}, u32[]{:S(2)}) collective-permute-start(bf16[128,1024]{1,0:T(8,128)(2,1)} %collective-permute-done.3.refs_5_), channel_id=1, source_target_pairs={{0,6},{2,0},{4,2},{6,4},{1,7},{3,1},{5,3},{7,5},{8,14},{10,8},{12,... | collective-permute-start | bytes 786440 | tf_op jit(solution)/shard_map/ppermute | solution.py:163
  144.7 0.7 copy-start.1
  145.4 1.0 copy-start.2
  174.6 38.4 %copy-start = (bf16[2048,384]{1,0:T(8,128)(2,1)S(1)}, bf16[2048,384]{1,0:T(8,128)(2,1)}, u32[]{:S(2)}) copy-start(bf16[2048,384]{1,0:T(8,128)(2,1)} %all-gather.4.cloned.1.call-done) | copy-start | bytes 4718596
  190.8 7.0 %collective-permute-start.7 = (f32[32,256]{1,0:T(8,128)S(1)}, f32[32,256]{1,0:T(8,128)S(1)}, u32[]{:S(2)}, u32[]{:S(2)}) collective-permute-start(f32[32,256]{1,0:T(8,128)S(1)} %reduce_sum.19), channel_id=1, source_target_pairs={{1,64},{64,1},{129,192},{192,129},{257,320},{320,257},{385,448},{4... | collective-permute-start | bytes 98312 | tf_op jit(solution)/shard_map/ppermute | solution.py:179
  209.7 3.2 %collective-permute-start.8 = (f32[4,32,256]{2,1,0:T(8,128)S(1)}, f32[4,32,256]{2,1,0:T(8,128)S(1)}, u32[]{:S(2)}, u32[]{:S(2)}) collective-permute-start(f32[4,32,256]{2,1,0:T(8,128)S(1)} %all_to_all.27), channel_id=1, source_target_pairs={{0,1},{1,0},{2,3},{3,2},{4,5},{5,4},{6,7},{7,6},{8,9},{9,8},{10,11... | collective-permute-start | bytes 393224 | tf_op jit(solution)/shard_map/ppermute | solution.py:167
Sparse Core Ops, SparseCore 0:
  70.6 39.2 all-gather.3

commit v5 on v3

--- a/solution.py
+++ b/solution.py
@@ -233,7 +233,7 @@
     term = gram(loss_weight, blocks, mixed_pair, lax.axis_size(NEAR), weight_all[:16, :HEAD])
     summed = reduce_near(term).reshape(lax.axis_size("y"), -1, mixed.shape[1])
     summed = settle(jnp.sum(exchange(summed, "y"), axis=0))
-    rows = exchange(jnp.broadcast_to(summed[None], (seq_count,) + summed.shape), SEQ)
+    rows = lax.all_gather(summed, SEQ, axis=0)
     total_tokens = length * dp_count
     return finish(
         rows, weight_all.reshape(seq_count, mixed.shape[1], -1), LOSS_SCALE / total_tokens**0.5

time: 223 us -> 221 us (level)
    all_to_all x3 -> x2, blocking collectives: 54.6 us -> 39.4 us  [exchange(): return lax.all_to_all(x, axes, split_axis=0, concat_axis=0, tiled=True)]
    all_gather x0 -> x1, blocking collectives: none -> 13.8 us  [shards(): rows = lax.all_gather(summed, SEQ, axis=0)]
where the time goes in v5:
time: 221 us; the launch traced here: 219 us
  blocking collectives  85.4 us (39%)
  starting transfers between devices  50.8 us (23%)
  waiting for transfers between devices  30.3 us (14%)
  Pallas kernels  23.2 us (10%)
  between operations  15.6 us (7%)
  local copies, waits for them, and re-layouts  9.58 us (4%)
  other arithmetic  4.62 us (2%)
    all_to_all x2, blocking collectives, exchange(): return lax.all_to_all(x, axes, split_axis=0, concat_axis=0, tiled=True)  39.4 us
    ppermute x6, waiting for transfers between devices, shift(): return lax.ppermute(x, 'zh', [(i, (i + step) % n) for i in range(n)])  23 us
    ppermute x6, starting transfers between devices, shift(): return lax.ppermute(x, 'zh', [(i, (i + step) % n) for i in range(n)])  22.2 us
    all_gather x1, blocking collectives, shards(): weight_part = lax.all_gather(weight_part, 'zl', axis=1)  21.9 us
    all_to_all x2, starting transfers between devices, exchange(): return lax.all_to_all(x, axes, split_axis=0, concat_axis=0, tiled=True)  18.5 us
    all_gather x1, blocking collectives, shards(): rows = lax.all_gather(summed, SEQ, axis=0)  13.8 us
    pallas_call x1, Pallas kernels, attend_tangent(): pl.pallas_call(functools.partial(tangent_kernel, scale), grid=(width // H...  11 us
    all_gather x1, blocking collectives, shards(): weight_part = lax.all_gather(out_weight, 'x', axis=0)  10.3 us
  transfers between devices with their start and end apart: 11, of which 5 were waited for; matrix products, arithmetic and copies ran while one was open for 3% of the time, Pallas kernels for 9%

profile of v5, /device:TPU:1, one launch (start us, length us, event | category | flops | bytes accessed | tf_op | source)
XLA Modules:
  0.0 219.5 jit_solution(6980200965273587943)
XLA Ops:
  6.5 1.4 copy.26
  7.9 0.2 copy.27
  8.2 0.3 copy.22
  8.4 0.2 copy.23
  8.7 0.3 copy-done.4
  9.0 0.3 copy.24
  9.2 0.2 copy.25
  9.5 1.3 pad_maximum_fusion
  10.8 11.9 %all-to-all-start = ((bf16[8,3,128,256]{3,2,1,0:T(8,128)(2,1)}), bf16[8,3,128,256]{3,2,1,0:T(8,128)(2,1)S(1)}, u32[]{:S(2)}, u32[]{:S(2)}) async-start(bf16[8,3,128,256]{3,2,1,0:T(8,128)(2,1)} %pad_maximum_fusion), calls=%async_computation | async-start | bytes 3145728 | tf_op jit(solution)/shard_map/all_to_all | solution.py:185
  22.7 0.3 copy.28
  23.0 0.2 copy.29
  23.2 0.5 copy-done.6
  23.8 0.3 copy.30
  24.1 0.2 copy.31
  24.3 1.3 copy.32
  25.6 1.0 copy.33
  26.6 10.3 %all-gather = bf16[128,384]{1,0:T(8,128)(2,1)S(1)} all-gather(bf16[32,384]{1,0:T(8,128)(2,1)S(1)} %copy-done.7), channel_id=2, replica_groups=mesh['y'=8,'x'=4,'zl'=2,'zh'=4,'core'=2] {'x'}, dimensions={0}, use_global_device_ids=true | all-gather | bytes 122880 | tf_op jit(solution)/shard_map/all_gather | solution.py:213
  36.9 2.3 %pad_maximum_fusion.1 = bf16[8,3,128,256]{3,2,1,0:T(8,128)(2,1)} fusion(bf16[8,1,128,256]{3,2,1,0:T(8,128)(2,1)} %bitcast.44, bf16[8,1,128,256]{3,2,1,0:T(8,128)(2,1)S(1)} %bitcast.42, bf16[8,1,128,256]{3,2,1,0:T(8,128)(2,1)S(1)} %bitcast.40), kind=kLoop, calls=%fused_computation.4 | loop fusion | flops 1572864 | bytes 3145728 | tf_op jit(solution)/shard_map/stack | solution.py:189
  39.2 21.9 %all-gather.1 = bf16[4,64,384]{2,1,0:T(8,128)(2,1)} all-gather(bf16[4,32,384]{2,1,0:T(8,128)(2,1)S(1)} %bitcast.48), channel_id=3, replica_groups=mesh['y'=8,'x'=4,'zl'=2,'zh'=4,'core'=2] {'zl'}, dimensions={1}, use_global_device_ids=true | all-gather | bytes 294912 | tf_op jit(solution)/shard_map/all_gather | solution.py:215
  61.2 6.6 %all-to-all-start.1 = ((bf16[8,3,128,256]{3,2,1,0:T(8,128)(2,1)}), bf16[8,3,128,256]{3,2,1,0:T(8,128)(2,1)S(1)}, u32[]{:S(2)}, u32[]{:S(2)}) async-start(bf16[8,3,128,256]{3,2,1,0:T(8,128)(2,1)} %pad_maximum_fusion.1), calls=%async_computation.1 | async-start | bytes 3145728 | tf_op jit(solution)/shard_map/all_to_all | solution.py:185
  67.7 0.7 all-gather.5.cloned.1.call-update
  69.1 3.8 %attend.2.refs_0_ = bf16[128,1024]{1,0:T(8,128)(2,1)S(1)} custom-call(bf16[8,3,128,256]{3,2,1,0:T(8,128)(2,1)S(1)} %all-to-all-done.q_ref.k_ref.v_ref, bf16[8,3,128,256]{3,2,1,0:T(8,128)(2,1)S(1)} %all-to-all-done.q_ref.k_ref.v_ref, bf16[8,3,128,256]{3,2,1,0:T(8,128)(2,1)S(1)} %all-to-all-done.q_ref.k_ref.v_ref), custom_call_target="tpu_custom_call" | custom-call | flops 536870912 | bytes 2097152 | tf_op jit(solution)/shard_map/attend/pallas_call | solution.py:75
  72.9 4.2 %collective-permute-start = (bf16[128,1024]{1,0:T(8,128)(2,1)S(1)}, bf16[128,1024]{1,0:T(8,128)(2,1)}, u32[]{:S(2)}, u32[]{:S(2)}) collective-permute-start(bf16[128,1024]{1,0:T(8,128)(2,1)S(1)} %attend.2.refs_0_), channel_id=1, source_target_pairs={{0,2},{2,4},{4,6},{6,0},{1,3},{3,5},{5,7},{7,1},{8,10},{10,12},{12... | collective-permute-start | bytes 786440 | tf_op jit(solution)/shard_map/ppermute | solution.py:163
  77.1 3.2 %collective-permute-start.2 = (bf16[128,1024]{1,0:T(8,128)(2,1)S(1)}, bf16[128,1024]{1,0:T(8,128)(2,1)}, u32[]{:S(2)}, u32[]{:S(2)}) collective-permute-start(bf16[128,1024]{1,0:T(8,128)(2,1)S(1)} %attend.2.refs_0_), channel_id=1, source_target_pairs={{0,6},{2,0},{4,2},{6,4},{1,7},{3,1},{5,3},{7,5},{8,14},{10,8},{12,... | collective-permute-start | bytes 786440 | tf_op jit(solution)/shard_map/ppermute | solution.py:163
  80.3 4.4 %attend.3.refs_1_ = bf16[128,1024]{1,0:T(8,128)(2,1)} custom-call(bf16[8,3,128,256]{3,2,1,0:T(8,128)(2,1)S(1)} %all-to-all-done.q_ref.k_ref.v_ref, bf16[8,3,128,256]{3,2,1,0:T(8,128)(2,1)S(1)} %all-to-all-done.q_ref.k_ref.v_ref, bf16[8,3,128,256]{3,2,1,0:T(8,128)(2,1)S(1)} %all-to-all-done.q_ref.k_ref.v_ref), custom_call_target="tpu_custom_call" | custom-call | flops 536870912 | bytes 2097152 | tf_op jit(solution)/shard_map/attend/pallas_call | solution.py:75
  84.7 3.9 %collective-permute-start.1 = (bf16[128,1024]{1,0:T(8,128)(2,1)}, bf16[128,1024]{1,0:T(8,128)(2,1)}, u32[]{:S(2)}, u32[]{:S(2)}) collective-permute-start(bf16[128,1024]{1,0:T(8,128)(2,1)} %attend.3.refs_1_), channel_id=1, source_target_pairs={{0,2},{2,4},{4,6},{6,0},{1,3},{3,5},{5,7},{7,1},{8,10},{10,12},{12... | collective-permute-start | bytes 786440 | tf_op jit(solution)/shard_map/ppermute | solution.py:163
  88.6 3.5 %collective-permute-start.3 = (bf16[128,1024]{1,0:T(8,128)(2,1)}, bf16[128,1024]{1,0:T(8,128)(2,1)}, u32[]{:S(2)}, u32[]{:S(2)}) collective-permute-start(bf16[128,1024]{1,0:T(8,128)(2,1)} %attend.3.refs_1_), channel_id=1, source_target_pairs={{0,6},{2,0},{4,2},{6,4},{1,7},{3,1},{5,3},{7,5},{8,14},{10,8},{12,... | collective-permute-start | bytes 786440 | tf_op jit(solution)/shard_map/ppermute | solution.py:163
  92.1 4.9 %all-to-all-done.1.dq_ref.dk_ref.dv_ref = bf16[8,3,128,256]{3,2,1,0:T(8,128)(2,1)S(1)} async-done(((bf16[8,3,128,256]{3,2,1,0:T(8,128)(2,1)}), bf16[8,3,128,256]{3,2,1,0:T(8,128)(2,1)S(1)}, u32[]{:S(2)}, u32[]{:S(2)}) %all-to-all-start.1) | async-done | bytes 1572896 | tf_op jit(solution)/shard_map/all_to_all | solution.py:185
  97.0 11.0 %tangent.1.refs_8_ = bf16[1024,256]{1,0:T(8,128)(2,1)} custom-call(f32[1]{0:T(128)S(6)} %copy.34.coef_ref, bf16[8,3,128,256]{3,2,1,0:T(8,128)(2,1)S(1)} %all-to-all-done.q_ref.k_ref.v_ref, bf16[8,3,128,256]{3,2,1,0:T(8,128)(2,1)S(1)} %all-to-all-done.q_ref.k_ref.v_ref, bf16[8,3,128,256]{3,2,1,0:T(8,128)(2,1)S(1)} %all-to-all-done.q_ref.k_ref.v_ref, ...), custom_call_target="tpu_custom_call" | custom-call | flops 3758096384 | bytes 8388608 | tf_op jit(solution)/shard_map/tangent/pallas_call | solution.py:92
  108.1 2.2 collective-permute-done.1.refs_3_
  110.3 11.9 %collective-permute-done.3.refs_5_ = bf16[128,1024]{1,0:T(8,128)(2,1)} collective-permute-done((bf16[128,1024]{1,0:T(8,128)(2,1)}, bf16[128,1024]{1,0:T(8,128)(2,1)}, u32[]{:S(2)}, u32[]{:S(2)}) %collective-permute-start.3) | collective-permute-done | bytes 262176 | tf_op jit(solution)/shard_map/ppermute | solution.py:163
  122.2 4.7 %collective-permute-start.6 = (bf16[1024,256]{1,0:T(8,128)(2,1)}, bf16[1024,256]{1,0:T(8,128)(2,1)S(1)}, u32[]{:S(2)}, u32[]{:S(2)}) collective-permute-start(bf16[1024,256]{1,0:T(8,128)(2,1)} %tangent.1.refs_8_), channel_id=1, source_target_pairs={{0,1},{1,0},{2,3},{3,2},{4,5},{5,4},{6,7},{7,6},{8,9},{9,8},{10,11... | collective-permute-start | bytes 1572872 | tf_op jit(solution)/shard_map/ppermute | solution.py:167
  126.9 4.3 %collective-permute-start.4 = (bf16[128,1024]{1,0:T(8,128)(2,1)}, bf16[128,1024]{1,0:T(8,128)(2,1)S(1)}, u32[]{:S(2)}, u32[]{:S(2)}) collective-permute-start(bf16[128,1024]{1,0:T(8,128)(2,1)} %collective-permute-done.refs_2_), channel_id=1, source_target_pairs={{0,2},{2,4},{4,6},{6,0},{1,3},{3,5},{5,7},{7,1},{8,10},{10,12},{12... | collective-permute-start | bytes 786440 | tf_op jit(solution)/shard_map/ppermute | solution.py:163
  131.2 3.1 %collective-permute-start.5 = (bf16[128,1024]{1,0:T(8,128)(2,1)}, bf16[128,1024]{1,0:T(8,128)(2,1)S(1)}, u32[]{:S(2)}, u32[]{:S(2)}) collective-permute-start(bf16[128,1024]{1,0:T(8,128)(2,1)} %collective-permute-done.3.refs_5_), channel_id=1, source_target_pairs={{0,6},{2,0},{4,2},{6,4},{1,7},{3,1},{5,3},{7,5},{8,14},{10,8},{12,... | collective-permute-start | bytes 786440 | tf_op jit(solution)/shard_map/ppermute | solution.py:163
  135.1 0.7 slice.16.refs_10_
  135.7 8.9 %collective-permute-done.4.refs_6_ = bf16[128,1024]{1,0:T(8,128)(2,1)S(1)} collective-permute-done((bf16[128,1024]{1,0:T(8,128)(2,1)}, bf16[128,1024]{1,0:T(8,128)(2,1)S(1)}, u32[]{:S(2)}, u32[]{:S(2)}) %collective-permute-start.4) | collective-permute-done | bytes 262176 | tf_op jit(solution)/shard_map/ppermute | solution.py:163
  144.7 0.7 copy-done.1
  145.4 0.9 copy-done.2
  146.3 2.8 %gram.1 = f32[8,264,256]{2,1,0:T(8,128)S(1)} custom-call(f32[1]{0:T(128)S(6)} %copy.35.weight_ref, s32[2]{0:T(128)S(1)} %pad_add_fusion.at_ref, bf16[128,1024]{1,0:T(8,128)(2,1)S(1)} %attend.2.refs_0_, bf16[128,1024]{1,0:T(8,128)(2,1)} %attend.3.refs_1_, bf16[128,1024]{1,0:T(8,128)(2,1)} %collective-permute-done.refs_2_, ...), custom_call_target="tpu_custom_call" | custom-call | tf_op jit(solution)/shard_map/gram/pallas_call | solution.py:133
  149.2 0.5 slice.17
  150.4 0.3 select_convert_fusion
  150.7 23.2 %all_to_all.20 = f16[8,264,256]{2,1,0:T(8,128)(2,1)S(1)} all-to-all(f16[8,264,256]{2,1,0:T(8,128)(2,1)S(1)} %select_convert_fusion), channel_id=1, replica_groups=mesh['y'=8,'x'=4,'zl'=2,'zh'=4,'core'=2] {'x','zl'}, dimensions={0} | all-to-all | bytes 2162688 | tf_op jit(solution)/shard_map/all_to_all | solution.py:185
  174.1 0.2 fusion
  174.4 16.2 %all_to_all.21 = f32[8,32,256]{2,1,0:T(8,128)S(1)} all-to-all(f32[8,32,256]{2,1,0:T(8,128)S(1)} %bitcast.46), channel_id=1, replica_groups=mesh['y'=8,'x'=4,'zl'=2,'zh'=4,'core'=2] {'y'}, dimensions={0} | all-to-all | bytes 524288 | tf_op jit(solution)/shard_map/all_to_all | solution.py:185
  190.6 5.4 %collective-permute-start.7 = (f32[32,256]{1,0:T(8,128)S(1)}, f32[32,256]{1,0:T(8,128)S(1)}, u32[]{:S(2)}, u32[]{:S(2)}) collective-permute-start(f32[32,256]{1,0:T(8,128)S(1)} %reduce_sum.19), channel_id=1, source_target_pairs={{1,64},{64,1},{129,192},{192,129},{257,320},{320,257},{385,448},{4... | collective-permute-start | bytes 98312 | tf_op jit(solution)/shard_map/ppermute | solution.py:179
  196.1 1.6 collective-permute-done.7
  197.7 13.8 %all-gather.2 = f32[256,256]{1,0:T(8,128)S(1)} all-gather(f32[32,256]{1,0:T(8,128)S(1)} %broadcast_select_fusion), channel_id=4, replica_groups=mesh['y'=8,'x'=4,'zl'=2,'zh'=4,'core'=2] {'zh','core'}, dimensions={0}, use_global_device_ids=true | all-gather | bytes 294912 | tf_op jit(solution)/shard_map/all_gather | solution.py:236
  211.5 1.2 finish.1
  (25 shorter events, 0.5 us)
Async XLA Ops:
  6.5 1.6 copy-start.3
  7.9 1.0 copy-start.4
  10.8 11.9 %copy-start.5 = (bf16[128,2048]{1,0:T(8,128)(2,1)S(1)}, bf16[128,2048]{1,0:T(8,128)(2,1)}, u32[]{:S(2)}) copy-start(bf16[128,2048]{1,0:T(8,128)(2,1)} %param.12) | copy-start | bytes 1572868
  10.8 50.4 %all-to-all-start = ((bf16[8,3,128,256]{3,2,1,0:T(8,128)(2,1)}), bf16[8,3,128,256]{3,2,1,0:T(8,128)(2,1)S(1)}, u32[]{:S(2)}, u32[]{:S(2)}) async-start(bf16[8,3,128,256]{3,2,1,0:T(8,128)(2,1)} %pad_maximum_fusion), calls=%async_computation | async-start | bytes 3145728 | tf_op jit(solution)/shard_map/all_to_all | solution.py:185
  22.7 1.0 copy-start.6
  24.1 2.6 %copy-start.7 = (bf16[32,384]{1,0:T(8,128)(2,1)S(1)}, bf16[32,384]{1,0:T(8,128)(2,1)}, u32[]{:S(2)}) copy-start(bf16[32,384]{1,0:T(8,128)(2,1)} %param.15) | copy-start | bytes 73732
  61.2 35.9 %all-to-all-start.1 = ((bf16[8,3,128,256]{3,2,1,0:T(8,128)(2,1)}), bf16[8,3,128,256]{3,2,1,0:T(8,128)(2,1)S(1)}, u32[]{:S(2)}, u32[]{:S(2)}) async-start(bf16[8,3,128,256]{3,2,1,0:T(8,128)(2,1)} %pad_maximum_fusion.1), calls=%async_computation.1 | async-start | bytes 3145728 | tf_op jit(solution)/shard_map/all_to_all | solution.py:185
  67.7 67.3 %all-gather.5.cloned.1.call-start = ((), (), s32[]{:S(2)}) async-start(), calls=%async_computation.4 | async-start | bytes 1769472 | tf_op jit(solution)/shard_map/all_gather | solution.py:218
  72.9 35.1 %collective-permute-start = (bf16[128,1024]{1,0:T(8,128)(2,1)S(1)}, bf16[128,1024]{1,0:T(8,128)(2,1)}, u32[]{:S(2)}, u32[]{:S(2)}) collective-permute-start(bf16[128,1024]{1,0:T(8,128)(2,1)S(1)} %attend.2.refs_0_), channel_id=1, source_target_pairs={{0,2},{2,4},{4,6},{6,0},{1,3},{3,5},{5,7},{7,1},{8,10},{10,12},{12... | collective-permute-start | bytes 786440 | tf_op jit(solution)/shard_map/ppermute | solution.py:163
  77.1 33.1 %collective-permute-start.2 = (bf16[128,1024]{1,0:T(8,128)(2,1)S(1)}, bf16[128,1024]{1,0:T(8,128)(2,1)}, u32[]{:S(2)}, u32[]{:S(2)}) collective-permute-start(bf16[128,1024]{1,0:T(8,128)(2,1)S(1)} %attend.2.refs_0_), channel_id=1, source_target_pairs={{0,6},{2,0},{4,2},{6,4},{1,7},{3,1},{5,3},{7,5},{8,14},{10,8},{12,... | collective-permute-start | bytes 786440 | tf_op jit(solution)/shard_map/ppermute | solution.py:163
  84.7 25.5 %collective-permute-start.1 = (bf16[128,1024]{1,0:T(8,128)(2,1)}, bf16[128,1024]{1,0:T(8,128)(2,1)}, u32[]{:S(2)}, u32[]{:S(2)}) collective-permute-start(bf16[128,1024]{1,0:T(8,128)(2,1)} %attend.3.refs_1_), channel_id=1, source_target_pairs={{0,2},{2,4},{4,6},{6,0},{1,3},{3,5},{5,7},{7,1},{8,10},{10,12},{12... | collective-permute-start | bytes 786440 | tf_op jit(solution)/shard_map/ppermute | solution.py:163
  88.6 33.5 %collective-permute-start.3 = (bf16[128,1024]{1,0:T(8,128)(2,1)}, bf16[128,1024]{1,0:T(8,128)(2,1)}, u32[]{:S(2)}, u32[]{:S(2)}) collective-permute-start(bf16[128,1024]{1,0:T(8,128)(2,1)} %attend.3.refs_1_), channel_id=1, source_target_pairs={{0,6},{2,0},{4,2},{6,4},{1,7},{3,1},{5,3},{7,5},{8,14},{10,8},{12,... | collective-permute-start | bytes 786440 | tf_op jit(solution)/shard_map/ppermute | solution.py:163
  122.2 23.2 %collective-permute-start.6 = (bf16[1024,256]{1,0:T(8,128)(2,1)}, bf16[1024,256]{1,0:T(8,128)(2,1)S(1)}, u32[]{:S(2)}, u32[]{:S(2)}) collective-permute-start(bf16[1024,256]{1,0:T(8,128)(2,1)} %tangent.1.refs_8_), channel_id=1, source_target_pairs={{0,1},{1,0},{2,3},{3,2},{4,5},{5,4},{6,7},{7,6},{8,9},{9,8},{10,11... | collective-permute-start | bytes 1572872 | tf_op jit(solution)/shard_map/ppermute | solution.py:167
  126.9 17.8 %collective-permute-start.4 = (bf16[128,1024]{1,0:T(8,128)(2,1)}, bf16[128,1024]{1,0:T(8,128)(2,1)S(1)}, u32[]{:S(2)}, u32[]{:S(2)}) collective-permute-start(bf16[128,1024]{1,0:T(8,128)(2,1)} %collective-permute-done.refs_2_), channel_id=1, source_target_pairs={{0,2},{2,4},{4,6},{6,0},{1,3},{3,5},{5,7},{7,1},{8,10},{10,12},{12... | collective-permute-start | bytes 786440 | tf_op jit(solution)/shard_map/ppermute | solution.py:163
  131.2 13.5 %collective-permute-start.5 = (bf16[128,1024]{1,0:T(8,128)(2,1)}, bf16[128,1024]{1,0:T(8,128)(2,1)S(1)}, u32[]{:S(2)}, u32[]{:S(2)}) collective-permute-start(bf16[128,1024]{1,0:T(8,128)(2,1)} %collective-permute-done.3.refs_5_), channel_id=1, source_target_pairs={{0,6},{2,0},{4,2},{6,4},{1,7},{3,1},{5,3},{7,5},{8,14},{10,8},{12,... | collective-permute-start | bytes 786440 | tf_op jit(solution)/shard_map/ppermute | solution.py:163
  144.7 0.7 copy-start.1
  145.4 1.0 copy-start.2
  174.1 37.3 %copy-start = (bf16[2048,384]{1,0:T(8,128)(2,1)S(1)}, bf16[2048,384]{1,0:T(8,128)(2,1)}, u32[]{:S(2)}) copy-start(bf16[2048,384]{1,0:T(8,128)(2,1)} %all-gather.5.cloned.1.call-done) | copy-start | bytes 4718596
  190.6 7.0 %collective-permute-start.7 = (f32[32,256]{1,0:T(8,128)S(1)}, f32[32,256]{1,0:T(8,128)S(1)}, u32[]{:S(2)}, u32[]{:S(2)}) collective-permute-start(f32[32,256]{1,0:T(8,128)S(1)} %reduce_sum.19), channel_id=1, source_target_pairs={{1,64},{64,1},{129,192},{192,129},{257,320},{320,257},{385,448},{4... | collective-permute-start | bytes 98312 | tf_op jit(solution)/shard_map/ppermute | solution.py:179
Sparse Core Ops, SparseCore 0:
  70.6 39.3 all-gather.4
